TPU v7x, 256 devices: a whole 4x4x8 slice. The times are simulated.
256 devices in a mesh: dp: 16 (over z, x_hi), mp: 16 (over y, x_lo, core).
Axes of the slice: x: 4 (x_hi: 2, x_lo: 2; x = x_hi * 2 + x_lo), y: 4, z: 8, core: 2. Of those that a mesh axis runs over, the one named last changes fastest.
Arguments:
- inputs: bfloat16 [4096, 4096], P('dp', 'mp'), may hold values from -50 to 50
- cotangent: bfloat16 [4096, 4096], P('dp', 'mp'), may hold values from -50 to 50
- w_up: bfloat16 [4096, 16384], P('dp', 'mp'), may hold values from -0.09375 to 0.09375
- w_down: bfloat16 [16384, 4096], P('mp', 'dp'), may hold values from -0.046875 to 0.046875
Outputs:
- input_grad: bfloat16 [4096, 4096], P('dp', 'mp')
- up_grad: float32 [4096, 16384], P('dp', 'mp')
- down_grad: float32 [16384, 4096], P('mp', 'dp')
- mean_square: float32 [], replicated
All inputs are finite; a program needn't handle non-finite values.
Results may differ from a plain program's by a relative error of at most 0.018.
Values may be sent and summed in bfloat16 or wider, within the bound.
A program may use at most 128 MiB of HBM per device.

v0:
```python
import jax
import jax.numpy as jnp
from jax import lax
from jax.sharding import PartitionSpec as P

D = 4096
FF = 16384


root_half = 0.7071067811865476
inv_root_two_pi = 0.3989422804014327


def gelu_value(hidden):
    return 0.5 * hidden * (1.0 + jax.scipy.special.erf(hidden * root_half))


def gelu_slope(hidden):
    return (
        0.5 * (1.0 + jax.scipy.special.erf(hidden * root_half))
        + hidden * jnp.exp(-0.5 * hidden * hidden) * inv_root_two_pi
    )


def contract_last(left, right):
    return lax.dot_general(
        left, right, (((1,), (1,)), ((), ())), preferred_element_type=jnp.float32
    )


def contract_first(left, right):
    return lax.dot_general(
        left, right, (((0,), (0,)), ((), ())), preferred_element_type=jnp.float32
    )


def on_device(inputs, cotangent, w_up, w_down):
    x_full, dy_full = (
        lax.all_gather(inputs, "mp", axis=1, tiled=True),
        lax.all_gather(cotangent, "mp", axis=1, tiled=True),
    )
    up_all, down_all = (
        lax.all_gather(w_up, "dp", axis=0, tiled=True),
        lax.all_gather(w_down, "dp", axis=1, tiled=True),
    )
    hidden = jnp.dot(x_full, up_all, preferred_element_type=jnp.float32)
    grad_act = contract_last(dy_full, down_all)
    act = gelu_value(hidden).astype(jnp.bfloat16)
    grad_pre = (grad_act * gelu_slope(hidden)).astype(jnp.bfloat16)
    grad_cols = lax.psum_scatter(
        contract_last(up_all, grad_pre), "mp", scatter_dimension=0, tiled=True
    )
    input_grad = grad_cols.T.astype(jnp.bfloat16)
    raw_up = lax.psum_scatter(
        contract_first(x_full, grad_pre).astype(jnp.bfloat16), "dp", scatter_dimension=0, tiled=True
    ).astype(jnp.float32)
    raw_down = (
        lax.psum_scatter(
            contract_first(dy_full, act).astype(jnp.bfloat16), "dp", scatter_dimension=0, tiled=True
        )
        .astype(jnp.float32)
        .T
    )
    local_sq = jnp.sum(raw_up * raw_up) + jnp.sum(raw_down * raw_down)
    total_sq = lax.psum(local_sq, ("dp", "mp"))
    mean_square = total_sq / jnp.float32(2.0 * D * FF)
    scale = 1.0 / jnp.sqrt(mean_square)
    return (input_grad, raw_up * scale, raw_down * scale, mean_square)


def solution(mesh):
    placed = (P("dp", "mp"), P("dp", "mp"), P("dp", "mp"), P("mp", "dp"))
    return jax.shard_map(
        on_device,
        mesh=mesh,
        in_specs=placed,
        out_specs=(P("dp", "mp"), P("dp", "mp"), P("mp", "dp"), P()),
        check_vma=False,
    )
```

profile of v0, /device:TPU:1, one launch (start us, length us, event | category | flops | bytes accessed | tf_op | source)
XLA Modules:
  0.0 1000.9 jit_solution(400941806674713497)
XLA Ops:
  7.2 0.0 all-gather.9.cloned.1.call-start
  7.2 0.7 all-gather.9.cloned.1.call-update
  7.9 0.0 all-gather.11.cloned.1.call-start
  7.9 0.7 all-gather.11.cloned.1.call-update
  8.6 0.0 all-gather.5.cloned.1.call-start
  8.7 0.7 all-gather.5.cloned.1.call-update
  9.4 0.0 all-gather.7.cloned.1.call-start
  9.4 0.5 all-gather.7.cloned.1.call-update
  10.0 0.0 reduce-scatter.8.cloned.1.call-start
  10.0 43.7 %all-gather.9.cloned.1.call-done = bf16[256,4096]{1,0:T(8,128)(2,1)} async-done(((bf16[256,256]{1,0:T(8,128)(2,1)}), bf16[256,4096]{1,0:T(8,128)(2,1)}) %all-gather.9.cloned.1.call-update) | async-done | bytes 2097168 | tf_op jit(solution)/shard_map/all_gather | solution.py:39
  53.7 138.0 %all-gather.11.cloned.1.call-done = bf16[4096,1024]{1,0:T(8,128)(2,1)} async-done(((bf16[256,1024]{1,0:T(8,128)(2,1)}), bf16[4096,1024]{1,0:T(8,128)(2,1)}) %all-gather.11.cloned.1.call-update) | async-done | bytes 8388624 | tf_op jit(solution)/shard_map/all_gather | solution.py:43
  191.7 6.3 fusion.10
  198.1 32.8 %all-gather.5.cloned.1.call-done = bf16[256,4096]{1,0:T(8,128)(2,1)} async-done(((bf16[256,256]{1,0:T(8,128)(2,1)}), bf16[256,4096]{1,0:T(8,128)(2,1)}) %all-gather.5.cloned.1.call-update) | async-done | bytes 2097168 | tf_op jit(solution)/shard_map/all_gather | solution.py:40
  230.8 7.2 convert_bitcast_fusion
  238.1 0.0 reduce-scatter.8.cloned.1.call-update
  238.1 0.0 copy-start
  238.1 0.0 reduce-scatter.6.cloned.1.call-start
  238.1 140.5 %all-gather.7.cloned.1.call-done = bf16[1024,4096]{1,0:T(8,128)(2,1)} async-done(((bf16[1024,256]{1,0:T(8,128)(2,1)}), bf16[1024,4096]{1,0:T(8,128)(2,1)}) %all-gather.7.cloned.1.call-update) | async-done | bytes 8388624 | tf_op jit(solution)/shard_map/all_gather | solution.py:44
  378.6 6.6 fusion
  385.2 0.0 copy-start.1
  385.2 0.8 copy-done.1
  386.0 0.0 copy-done
  386.0 5.6 convert_bitcast_fusion.1
  391.6 0.0 copy-start.2
  391.6 0.0 reduce-scatter.6.cloned.1.call-update
  391.7 0.0 reduce-scatter.4.cloned.1.call-start
  391.7 1.0 copy-done.2
  392.7 8.1 convolution_bitcast_fusion
  400.8 0.0 reduce-scatter.4.cloned.1.call-update
  400.8 203.4 %reduce-scatter.8.cloned.1.call-done = bf16[256,1024]{0,1:T(8,128)(2,1)} async-done(((bf16[4096,1024]{0,1:T(8,128)(2,1)}), bf16[256,1024]{0,1:T(8,128)(2,1)}) %reduce-scatter.8.cloned.1.call-update) | async-done | bytes 524304 | tf_op jit(solution)/shard_map/reduce_scatter | solution.py:58
  604.2 1.9 fusion.2
  606.1 227.4 %reduce-scatter.6.cloned.1.call-done = bf16[256,1024]{0,1:T(8,128)(2,1)} async-done(((bf16[4096,1024]{0,1:T(8,128)(2,1)}), bf16[256,1024]{0,1:T(8,128)(2,1)}) %reduce-scatter.6.cloned.1.call-update) | async-done | bytes 524304 | tf_op jit(solution)/shard_map/reduce_scatter | solution.py:54
  833.5 1.9 fusion.1
  836.7 71.6 %reduce-scatter.4.cloned.1.call-done = f32[256,256]{0,1:T(8,128)} async-done(((f32[4096,256]{0,1:T(8,128)}), f32[256,256]{0,1:T(8,128)}) %reduce-scatter.4.cloned.1.call-update) | async-done | bytes 262160 | tf_op jit(solution)/shard_map/reduce_scatter | solution.py:50
  908.3 1.6 convert_bitcast_fusion.2
  909.9 78.7 %psum.7 = f32[]{:T(128)} all-reduce(f32[]{:T(128)S(6)} %add.20), channel_id=1, replica_groups=mesh['dp'=16,'mp'=16] {'dp','mp'}, use_global_device_ids=true, to_apply=%region_5.0 | all-reduce | flops 1 | bytes 8 | tf_op jit(solution)/shard_map/psum | solution.py:65
  989.3 2.3 convert_multiply_fusion.2
  991.7 1.3 copy.8
Async XLA Ops:
  7.2 46.5 %all-gather.9.cloned.1.call-start = ((), (), s32[]{:S(2)}) async-start(), calls=%async_computation.5 | async-start | bytes 2228224 | tf_op jit(solution)/shard_map/all_gather | solution.py:39
  7.9 183.8 %all-gather.11.cloned.1.call-start = ((), (), s32[]{:S(2)}) async-start(), calls=%async_computation.6 | async-start | bytes 8912896 | tf_op jit(solution)/shard_map/all_gather | solution.py:43
  8.6 222.2 %all-gather.5.cloned.1.call-start = ((), (), s32[]{:S(2)}) async-start(), calls=%async_computation.3 | async-start | bytes 2228224 | tf_op jit(solution)/shard_map/all_gather | solution.py:40
  9.4 369.3 %all-gather.7.cloned.1.call-start = ((), (), s32[]{:S(2)}) async-start(), calls=%async_computation.4 | async-start | bytes 8912896 | tf_op jit(solution)/shard_map/all_gather | solution.py:44
  10.0 594.2 %reduce-scatter.8.cloned.1.call-start = ((), (), s32[]{:S(2)}) async-start(), calls=%async_computation.9 | async-start | bytes 8912896 | tf_op jit(solution)/shard_map/reduce_scatter | solution.py:58
  238.1 147.9 %copy-start = (bf16[256,4096]{1,0:T(8,128)(2,1)S(1)}, bf16[256,4096]{1,0:T(8,128)(2,1)}, u32[]{:S(2)}) copy-start(bf16[256,4096]{1,0:T(8,128)(2,1)} %all-gather.9.cloned.1.call-done) | copy-start | bytes 6291460
  238.1 595.4 %reduce-scatter.6.cloned.1.call-start = ((), (), s32[]{:S(2)}) async-start(), calls=%async_computation.8 | async-start | bytes 8912896 | tf_op jit(solution)/shard_map/reduce_scatter | solution.py:54
  385.2 0.8 copy-start.1
  391.6 1.0 copy-start.2
  391.7 516.6 %reduce-scatter.4.cloned.1.call-start = ((), (), s32[]{:S(2)}) async-start(), calls=%async_computation.7 | async-start | bytes 4456448 | tf_op jit(solution)/shard_map/reduce_scatter | solution.py:50
Sparse Core Ops, SparseCore 0:
  9.8 43.8 all-gather.8
  56.3 135.3 all-gather.10
  193.5 37.3 all-gather.4
  233.2 145.4 all-gather.6
  382.6 221.5 reduce-scatter.7
  608.1 225.2 reduce-scatter.5
  836.0 72.1 reduce-scatter.3
where the time goes:
time: 1000 us
  waiting for transfers between devices  860 us (86%)
  blocking collectives  78.7 us (8%)
  matrix products  33.8 us (3%)
  between operations  17.3 us (2%)
    reduce_scatter x1, waiting for transfers between devices, on_device(): lax.psum_scatter(contract_first(x_full, grad_pre).astype(jnp.bfloat16), '...  227 us
    reduce_scatter x1, waiting for transfers between devices, on_device(): lax.psum_scatter(contract_first(dy_full, act).astype(jnp.bfloat16), 'dp',...  203 us
    all_gather x1, waiting for transfers between devices, on_device(): lax.all_gather(w_down, 'dp', axis=1, tiled=True)  140 us
    all_gather x1, waiting for transfers between devices, on_device(): lax.all_gather(w_up, 'dp', axis=0, tiled=True)  138 us
    psum x1, blocking collectives, on_device(): total_sq = lax.psum(local_sq, ('dp', 'mp'))  78.7 us
    reduce_scatter x1, waiting for transfers between devices, on_device(): lax.psum_scatter(contract_last(up_all, grad_pre), 'mp', scatter_dimension...  71.6 us
    all_gather x1, waiting for transfers between devices, on_device(): lax.all_gather(inputs, 'mp', axis=1, tiled=True)  43.7 us
    all_gather x1, waiting for transfers between devices, on_device(): lax.all_gather(cotangent, 'mp', axis=1, tiled=True)  32.8 us
  transfers between devices with their start and end apart: 7, of which 7 were waited for; matrix products, arithmetic and copies ran while one was open for 4% of the time, Pallas kernels for 0%

commit v1 on v0

v1 whole, which is shorter than its diff:
```python
import jax
import jax.numpy as jnp
from jax import lax
from jax.experimental import pallas as pl
from jax.experimental.pallas import tpu as pltpu
from jax.sharding import PartitionSpec as P

D = 4096
FF = 16384

NX, NY, NZ = 4, 4, 8
XT = 64
TZ = 2 * XT
TOK = NZ * TZ
KB = 256
UB = 128
UN = 2 * UB
ROW = NZ * KB
CUT = 768
NQ = 2
QR = UB // NQ

MESH = pl.DeviceIdType.MESH
BF = jnp.bfloat16
F32 = jnp.float32

root_half = 0.7071067811865476
inv_root_two_pi = 0.3989422804014327


def step(value, offset, size):
    return lax.rem(value + (offset + size), size)


def span(start, size):
    return pl.ds(pl.multiple_of(start, size), size)


def dot_nt(left, right):
    return lax.dot_general(
        left, right, (((1,), (1,)), ((), ())), preferred_element_type=F32
    )


def dot_nn(left, right):
    return lax.dot_general(
        left, right, (((1,), (0,)), ((), ())), preferred_element_type=F32
    )


def kernel(
    xy_in, w_in, ig_out, grad_out, sq_out,
    xy, ww, hid, gact, act_t, pre, pre_t,
    part, r1r, r1l, r2r, r2l, red, land,
    ig_send, ig_recv, py, y1r, y1l, y2r, y2l, ty, zl, fz, ox, nb,
    send, recv, local,
):
    dp, mp = lax.axis_index("dp"), lax.axis_index("mp")
    z, xh = lax.div(dp, 2), lax.rem(dp, 2)
    y, xl, c = lax.div(mp, 4), lax.rem(lax.div(mp, 2), 2), lax.rem(mp, 2)
    x = 2 * xh + xl

    def device(px, py_, pz, pc):
        return (pz * 2 + lax.div(px, 2), py_ * 4 + lax.rem(px, 2) * 2 + pc)

    def at_x(k):
        return device(step(x, k, NX), y, z, c)

    def at_y(k):
        return device(x, step(y, k, NY), z, c)

    def at_z(k):
        return device(x, y, step(z, k, NZ), c)

    sibling = device(x, y, z, 1 - c)

    started = []

    def push(src, dst, target):
        n = len(started)
        copy = pltpu.make_async_remote_copy(
            src_ref=src, dst_ref=dst, send_sem=send.at[n], recv_sem=recv.at[n],
            device_id=target, device_id_type=MESH,
        )
        copy.start()
        started.append(copy)
        return copy

    def land_all(copies):
        for copy in copies:
            copy.wait_recv()

    barrier = pltpu.get_barrier_semaphore()
    peers = (
        [at_x(k) for k in range(1, NX)]
        + [at_y(k) for k in range(1, NY)]
        + [at_z(k) for k in range(1, NZ)]
        + [sibling]
    )
    for peer in peers:
        pl.semaphore_signal(barrier, inc=1, device_id=peer, device_id_type=MESH)
    pl.semaphore_wait(barrier, len(peers))

    first, rest = pl.ds(0, CUT), pl.ds(CUT, 4 * KB - CUT)

    def rows(pz):
        return span(pz * TZ, TZ)

    def half(pz, which):
        return span(pz * TZ + which * XT, XT)

    def cols(pz):
        return span(pz * KB, KB)

    tok_place = xy.at[c, y, span(z * TZ + xh * XT, XT), span(xl * 2 * KB, 2 * KB)]
    tok_own = pltpu.make_async_copy(xy_in.at[span(x * XT, XT), :], tok_place, local.at[0])
    tok_own.start()
    tok = []
    for k in (1, 3, 2):
        px = step(x, k, NX)
        tok.append(push(xy_in.at[span(px * XT, XT), :], tok_place, at_x(k)))

    w_place = ww.at[x, :, :, cols(z)]
    w_own = pltpu.make_async_copy(w_in.at[:, span(z * UB, UB), :], w_place, local.at[1])
    w_own.start()
    wz = {}

    def w_send(k):
        pz = step(z, k, NZ)
        wz[k] = push(w_in.at[:, span(pz * UB, UB), :], w_place, at_z(k))

    for k in (1, 7, 2, 6):
        w_send(k)

    wx1, wx2 = {}, {}

    def w_hop1(k):
        piece = ww.at[x, :, :, cols(step(z, -k, NZ))]
        wx1[k] = [push(piece, piece, at_x(1)), push(piece, piece, at_x(-1))]

    def w_hop2(k):
        land_all(wx1[k])
        pz = cols(step(z, -k, NZ))
        right = ww.at[step(x, -1, NX), 0, :, pz]
        left = ww.at[step(x, 1, NX), 1, :, pz]
        wx2[k] = [push(right, right, at_x(1)), push(left, left, at_x(-1))]

    ya1, ya2, ca, cb, za, zb = {}, {}, {}, {}, {}, {}

    def ya_hop1(k):
        block = xy.at[c, y, rows(step(z, k, NZ)), first]
        ya1[k] = [push(block, block, at_y(1)), push(block, block, at_y(-1))]

    def ya_hop2(k):
        land_all(ya1[k])
        pz = step(z, k, NZ)
        right = xy.at[c, step(y, -1, NY), half(pz, 0), first]
        left = xy.at[c, step(y, 1, NY), half(pz, 1), first]
        ya2[k] = [push(right, right, at_y(1)), push(left, left, at_y(-1))]

    def ya_core(k):
        land_all(ya2[k])
        block = xy.at[c, :, rows(step(z, k, NZ)), first]
        ca[k] = push(block, block, sibling)

    def za_step(k):
        if k < 4:
            right = xy.at[c, y, rows(step(z, 1 - k, NZ)), first]
            left = xy.at[c, y, rows(step(z, k - 1, NZ)), first]
        else:
            right = xy.at[c, y, half(step(z, 1 - k, NZ), 0), first]
            left = xy.at[c, y, half(step(z, k - 1, NZ), 1), first]
        za[k] = [push(right, right, at_z(1)), push(left, left, at_z(-1))]

    def zb_step(k):
        if k < 4:
            right = xy.at[c, :, rows(step(z, 1 - k, NZ)), rest]
            left = xy.at[c, :, rows(step(z, k - 1, NZ)), rest]
        else:
            right = xy.at[c, :, half(step(z, 1 - k, NZ), 0), rest]
            left = xy.at[c, :, half(step(z, k - 1, NZ), 1), rest]
        zb[k] = [push(right, right, at_z(1)), push(left, left, at_z(-1))]

    def cb_core(k):
        block = xy.at[c, :, rows(step(z, k, NZ)), rest]
        cb[k] = push(block, block, sibling)

    tok_own.wait()
    land_all(tok)
    block = xy.at[c, y, rows(z), rest]
    yb1 = [push(block, block, at_y(1)), push(block, block, at_y(-1))]
    za_step(1)
    ya_hop1(0)
    w_own.wait()
    w_hop1(0)

    land_all(yb1)
    right = xy.at[c, step(y, -1, NY), half(z, 0), rest]
    left = xy.at[c, step(y, 1, NY), half(z, 1), rest]
    yb2 = [push(right, right, at_y(1)), push(left, left, at_y(-1))]
    land_all(za[1])
    za_step(2)
    ya_hop1(1)
    ya_hop1(-1)

    land_all(yb2)
    zb_step(1)
    cb_core(0)
    for k in (3, 5, 4):
        w_send(k)
    for k in (1, 7):
        wz[k].wait_recv()
        w_hop1(k)
    ya_hop2(0)

    land_all(za[2])
    za_step(3)
    ya_hop1(2)
    ya_hop1(-2)
    w_hop2(0)

    land_all(zb[1])
    zb_step(2)
    cb_core(1)
    cb_core(-1)
    for k in (2, 6):
        wz[k].wait_recv()
        w_hop1(k)
    ya_hop2(1)
    ya_hop2(-1)

    land_all(za[3])
    za_step(4)
    ya_hop1(3)
    ya_hop1(-3)
    w_hop2(1)
    w_hop2(7)
    ya_core(0)

    land_all(zb[2])
    zb_step(3)
    cb_core(2)
    cb_core(-2)
    for k in (3, 5):
        wz[k].wait_recv()
        w_hop1(k)
    ya_hop2(2)
    ya_hop2(-2)

    land_all(za[4])
    ya_hop1(4)
    w_hop2(2)
    w_hop2(6)
    ya_core(1)
    ya_core(-1)

    land_all(zb[3])
    zb_step(4)
    cb_core(3)
    cb_core(-3)
    wz[4].wait_recv()
    w_hop1(4)
    w_hop2(3)
    w_hop2(5)
    ya_hop2(3)
    ya_hop2(-3)
    w_hop2(4)
    ya_core(2)
    ya_core(-2)
    ya_hop2(4)
    land_all(zb[4])
    cb_core(4)
    ya_core(3)
    ya_core(-3)
    ya_core(4)
    for k in range(NZ):
        land_all(wx2[k])
    for k in ca:
        ca[k].wait_recv()
        cb[k].wait_recv()

    hid[...] = jnp.zeros_like(hid)
    gact[...] = jnp.zeros_like(gact)

    def weight(which, pc, start, size):
        return ww[pl.ds(2 * pc, 2), which, :, span(start, size)].reshape(UN, size)

    def operand(which, p):
        return xy[
            lax.div(p, NZ), lax.div(lax.rem(p, NZ), 2), :,
            span((2 * lax.rem(p, 2) + which) * KB, KB),
        ]

    @pl.loop(0, 16)
    def _(p):
        pc, start = lax.div(p, NZ), lax.rem(p, NZ) * KB
        hid[...] += dot_nt(operand(0, p), weight(0, pc, start, KB))
        gact[...] += dot_nt(operand(1, p), weight(1, pc, start, KB))

    @pl.loop(0, NZ)
    def _(t):
        at = span(t * TZ, TZ)
        h = hid[at, :]
        both = 0.5 * (1.0 + lax.erf(h * root_half))
        act = (h * both).astype(BF)
        slope = both + h * jnp.exp(-0.5 * h * h) * inv_root_two_pi
        grad = (gact[at, :] * slope).astype(BF)
        pre[at, :] = grad
        pre_t[:, at] = grad.T
        act_t[:, at] = act.T

    def ig_part(pc, py_, h, at):
        return dot_nn(pre[at, :], weight(0, pc, (2 * py_ + h) * KB, KB))

    igc = {}
    for k in (2, 1, -1, 0):
        py_ = step(y, k, NY)
        for h in range(2):
            @pl.loop(0, 4)
            def _(t):
                at = span(t * 256, 256)
                ig_send[py_, h, at, :] = ig_part(1 - c, py_, h, at).astype(BF)

            igc[k, h] = push(ig_send.at[py_, h], ig_recv.at[py_, h], sibling)

    def grad_parts(pc):
        @pl.loop(0, NZ)
        def _(q):
            p = pc * NZ + q
            for a, left in ((0, pre_t), (1, act_t)):
                out = dot_nn(left[...], operand(a, p)).astype(BF)
                part[2 * pc, a, :, cols(q)] = out[:UB]
                part[2 * pc + 1, a, :, cols(q)] = out[UB:]

    grad_parts(1 - xh)
    x1 = {}
    for q in range(NQ):
        at = pl.ds(q * QR, QR)
        far = step(x, 2, NX)
        x1[q] = [
            push(part.at[far, 0, at, :], r1r.at[q], at_x(1)),
            push(part.at[far, 1, at, :], r1l.at[q], at_x(-1)),
        ]

    def ig_own(py_, h, at):
        return ig_part(c, py_, h, at) + ig_recv[py_, h, at, :].astype(F32)

    y1 = {}
    for h in range(2):
        py_ = step(y, 2, NY)
        igc[2, h].wait_recv()

        @pl.loop(0, 4)
        def _(t):
            at = span(t * 256, 256)
            py[0, h, at, :] = ig_own(py_, h, at).astype(BF)

        y1[h] = [
            push(py.at[0, h, pl.ds(0, TOK // 2), :], y1r.at[h], at_y(1)),
            push(py.at[0, h, pl.ds(TOK // 2, TOK // 2), :], y1l.at[h], at_y(-1)),
        ]

    grad_parts(xh)

    x2 = {}
    for q in range(NQ):
        at = pl.ds(q * QR, QR)
        land_all(x1[q])
        nxt, prv = step(x, 1, NX), step(x, -1, NX)
        for px, a, got in ((nxt, 0, r1r), (prv, 1, r1l)):
            total = part[px, a, at, :].astype(F32) + got[q].astype(F32)
            part[px, a, at, :] = total.astype(BF)
        x2[q] = [
            push(part.at[nxt, :, at, :], r2r.at[q], at_x(1)),
            push(part.at[prv, :, at, :], r2l.at[q], at_x(-1)),
        ]

    y2 = {}
    for h in range(2):
        land_all(y1[h])
        for k, slot, mine, got in ((1, 1, 0, y1r), (-1, 2, 1, y1l)):
            py_ = step(y, k, NY)
            igc[k, h].wait_recv()
            for side in range(2):
                @pl.loop(0, 2)
                def _(t):
                    at = span(side * (TOK // 2) + t * 256, 256)
                    total = ig_own(py_, h, at)
                    if side == mine:
                        total = total + got[h, span(t * 256, 256), :].astype(F32)
                    py[slot, h, at, :] = total.astype(BF)

        y2[h] = [
            push(py.at[1, h], y2r.at[h], at_y(1)),
            push(py.at[2, h], y2l.at[h], at_y(-1)),
        ]

    gz, gz_own = [], []
    for q in range(NQ):
        at = pl.ds(q * QR, QR)
        land_all(x2[q])
        for a in range(2):
            total = (
                part[x, a, at, :].astype(F32)
                + r2r[q, a].astype(F32)
                + r2l[q, a].astype(F32)
            )
            red[q, a] = total.astype(BF)
        place = land.at[:, span(z * UB + q * QR, QR), :]
        own = pltpu.make_async_copy(red.at[q, :, :, cols(z)], place, local.at[2 + q])
        own.start()
        gz_own.append(own)
        for k in (1, 7, 2, 6, 3, 5, 4):
            gz.append(push(red.at[q, :, :, cols(step(z, k, NZ))], place, at_z(k)))

    iz = {}
    for h in range(2):
        land_all(y2[h])
        igc[0, h].wait_recv()

        @pl.loop(0, 4)
        def _(t):
            at = span(t * 256, 256)
            total = ig_own(y, h, at) + y2r[h, at, :].astype(F32) + y2l[h, at, :].astype(F32)
            ty[h, at, :] = total.astype(BF)

        zl[h, z] = ty[h, rows(z), :]
        iz[h] = [
            push(ty.at[h, rows(step(z, k, NZ)), :], zl.at[h, z], at_z(k))
            for k in (1, 7, 2, 6, 3, 5, 4)
        ]

    for copy in gz_own:
        copy.wait()
    land_all(gz)

    def square(t, total):
        for a in range(2):
            v = land[a, span(t * 64, 64), :].astype(F32)
            total = total + jnp.sum(v * v, axis=0, keepdims=True)
        return total

    squares = lax.fori_loop(0, 16, square, jnp.zeros((1, KB), F32))
    value = jnp.sum(squares, axis=1, keepdims=True)

    def exchange(stage, me, size, targets, value):
        nb[stage, me] = jnp.broadcast_to(value, (8, 128))
        return [push(nb.at[stage, me], nb.at[stage, me], t) for t in targets]

    def collect(stage, size, copies):
        land_all(copies)
        total = nb[stage, 0]
        for n in range(1, size):
            total = total + nb[stage, n]
        return total[:1, :1]

    norm = exchange(0, z, NZ, [at_z(k) for k in range(1, NZ)], value)

    for h in range(2):
        land_all(iz[h])
        total = zl[h, 0].astype(F32)
        for n in range(1, NZ):
            total = total + zl[h, n].astype(F32)
        fz[h] = total.astype(BF)

    def last(px):
        return fz.at[lax.rem(px, 2), span(lax.div(px, 2) * XT, XT), :]

    o_place = ox.at[span(x * XT, XT), :]
    o_own = pltpu.make_async_copy(last(x), o_place, local.at[2 + NQ])
    o_own.start()
    o_far = [push(last(step(x, k, NX)), o_place, at_x(k)) for k in (1, 3, 2)]

    value = collect(0, NZ, norm)
    norm = exchange(1, x, NX, [at_x(k) for k in range(1, NX)], value)
    grad_out[...] = land[...]
    value = collect(1, NX, norm)
    norm = exchange(2, y, NY, [at_y(k) for k in range(1, NY)], value)
    o_own.wait()
    land_all(o_far)
    ig_out[...] = ox[...]
    value = collect(2, NY, norm)
    norm = exchange(3, c, 2, [sibling], value)
    value = collect(3, 2, norm)
    sq_out[...] = jnp.broadcast_to(value, (8, 128))

    for copy in started:
        copy.wait_send()


def on_device(inputs, cotangent, w_up, w_down):
    xy = jnp.concatenate([inputs, cotangent], axis=1)
    w = jnp.stack([w_up.T, w_down])
    vmem = pl.BlockSpec(memory_space=pltpu.VMEM)
    hbm = pl.BlockSpec(memory_space=pl.ANY)
    ig, grads, total = pl.pallas_call(
        kernel,
        out_shape=(
            jax.ShapeDtypeStruct((NX * XT, KB), BF),
            jax.ShapeDtypeStruct((2, NZ * UB, KB), BF),
            jax.ShapeDtypeStruct((8, 128), F32),
        ),
        in_specs=[hbm, hbm],
        out_specs=(vmem, vmem, vmem),
        scratch_shapes=[
            pltpu.VMEM((2, NY, TOK, 4 * KB), BF),
            pltpu.VMEM((NX, 2, UB, ROW), BF),
            pltpu.VMEM((TOK, UN), F32),
            pltpu.VMEM((TOK, UN), F32),
            pltpu.VMEM((UN, TOK), BF),
            pltpu.VMEM((TOK, UN), BF),
            pltpu.VMEM((UN, TOK), BF),
            pltpu.VMEM((NX, 2, UB, ROW), BF),
            pltpu.VMEM((NQ, QR, ROW), BF),
            pltpu.VMEM((NQ, QR, ROW), BF),
            pltpu.VMEM((NQ, 2, QR, ROW), BF),
            pltpu.VMEM((NQ, 2, QR, ROW), BF),
            pltpu.VMEM((NQ, 2, QR, ROW), BF),
            pltpu.VMEM((2, NZ * UB, KB), BF),
            pltpu.VMEM((NY, 2, TOK, KB), BF),
            pltpu.VMEM((NY, 2, TOK, KB), BF),
            pltpu.VMEM((3, 2, TOK, KB), BF),
            pltpu.VMEM((2, TOK // 2, KB), BF),
            pltpu.VMEM((2, TOK // 2, KB), BF),
            pltpu.VMEM((2, TOK, KB), BF),
            pltpu.VMEM((2, TOK, KB), BF),
            pltpu.VMEM((2, TOK, KB), BF),
            pltpu.VMEM((2, NZ, TZ, KB), BF),
            pltpu.VMEM((2, TZ, KB), BF),
            pltpu.VMEM((NX * XT, KB), BF),
            pltpu.VMEM((4, NZ, 8, 128), F32),
            pltpu.SemaphoreType.DMA((200,)),
            pltpu.SemaphoreType.DMA((200,)),
            pltpu.SemaphoreType.DMA((8,)),
        ],
        compiler_params=pltpu.CompilerParams(
            collective_id=0, has_side_effects=True, vmem_limit_bytes=60 * 2**20
        ),
        cost_estimate=pl.CostEstimate(
            flops=11_000_000_000, bytes_accessed=8_000_000, transcendentals=524288
        ),
    )(xy, w)
    mean_square = total[0, 0] / jnp.float32(2.0 * D * FF)
    scale = 1.0 / jnp.sqrt(mean_square)
    up = grads[0].T.astype(F32) * scale
    down = grads[1].astype(F32) * scale
    return ig, up, down, mean_square


def solution(mesh):
    placed = (P("dp", "mp"), P("dp", "mp"), P("dp", "mp"), P("mp", "dp"))
    return jax.shard_map(
        on_device,
        mesh=mesh,
        in_specs=placed,
        out_specs=(P("dp", "mp"), P("dp", "mp"), P("mp", "dp"), P()),
        check_vma=False,
    )
```

time: 1000 us -> 199 us (0.20)
  waiting for transfers between devices: 860 us -> 0 us
  Pallas kernels: 0 us -> 186 us
  blocking collectives: 78.7 us -> 0 us
  matrix products: 33.8 us -> 0 us
  between operations: 17.3 us -> 2.48 us
    reduce_scatter x3 -> x0, waiting for transfers between devices: 502 us -> none  [the longest x1 227 us: on_device(): lax.psum_scatter(contract_first(x_full, grad_pre).astype(jnp.bfloat16), '...]
    all_gather x4 -> x0, waiting for transfers between devices: 355 us -> none  [the longest x1 140 us: on_device(): lax.all_gather(w_down, 'dp', axis=1, tiled=True)]
    pallas_call x0 -> x1, Pallas kernels: none -> 186 us  [on_device(): pl.pallas_call(kernel, out_shape=(jax.ShapeDtypeStruct((NX * XT, KB), BF)...]
    psum x1 -> x0, blocking collectives: 78.7 us -> none  [on_device(): total_sq = lax.psum(local_sq, ('dp', 'mp'))]
    dot_general x5 -> x0, matrix products: 33.8 us -> none  [the longest x2 14.7 us: contract_last(): lax.dot_general(left, right, (((1,), (1,)), ((), ())), preferred_element_...]
  transfers between devices with their start and end apart: 7 -> 0, of which waited for: 7 -> 0; matrix products, arithmetic and copies ran while one was open for 4% -> 0% of each run, Pallas kernels for 0% -> 0%
where the time goes in v1:
time: 199 us; the launch traced here: 198 us
  Pallas kernels  186 us (93%)
  other arithmetic  5.14 us (3%)
  local copies, waits for them, and re-layouts  4.19 us (2%)
  between operations  2.48 us (1%)
    pallas_call x1, Pallas kernels, on_device(): pl.pallas_call(kernel, out_shape=(jax.ShapeDtypeStruct((NX * XT, KB), BF)...  186 us

profile of v1, /device:TPU:1, one launch (start us, length us, event | category | flops | bytes accessed | tf_op | source)
XLA Modules:
  0.0 198.3 jit_solution(5891376151814081183)
XLA Ops:
  0.6 0.0 copy-start
  0.6 1.7 pad_maximum_fusion.1.xy_in
  2.4 0.0 copy-done
  2.4 0.0 copy-start.1
  2.4 0.2 copy.8
  2.6 0.8 copy-done.1
  3.4 1.1 pad_maximum_fusion.w_in
  4.5 186.5 %shard_map.75 = (bf16[256,256]{1,0:T(8,128)(2,1)}, bf16[2,1024,256]{2,1,0:T(8,128)(2,1)}, f32[8,128]{1,0:T(8,128)}) custom-call(bf16[256,512]{1,0:T(8,128)(2,1)} %pad_maximum_fusion.1.xy_in, bf16[2,1024,256]{2,1,0:T(8,128)(2,1)} %pad_maximum_fusion.w_in), custom_call_target="tpu_custom_call" | custom-call | flops 11000000512 | bytes 8000000 | tf_op jit(solution)/shard_map/pallas_call | solution.py:496
  191.0 1.2 slice.10
  192.8 2.3 %multiply_bitcast_fusion = (f32[1024,256]{1,0:T(8,128)}, f32[256,1024]{0,1:T(8,128)S(1)}) fusion(bf16[2,1024,256]{2,1,0:T(8,128)(2,1)} %get-tuple-element.8, f32[]{:T(128)S(6)} %sqrt.3), kind=kLoop, calls=%fused_computation.1 | loop fusion | flops 1048576 | bytes 3145732 | tf_op jit(solution)/shard_map/mul | solution.py:546
  195.2 0.0 copy-start.2
  195.2 1.3 copy.9
  196.5 0.0 copy-done.2
  196.5 0.7 copy.11
Async XLA Ops:
  0.6 1.8 copy-start
  2.4 1.0 copy-start.1
  195.2 1.3 copy-start.2

commit v2 on v1

v2 whole, which is shorter than its diff:
```python
import jax
import jax.numpy as jnp
from jax import lax
from jax.experimental import pallas as pl
from jax.experimental.pallas import tpu as pltpu
from jax.sharding import PartitionSpec as P

D = 4096
FF = 16384

NX, NY, NZ = 4, 4, 8
XT = 64
TZ = 2 * XT
TOK = NZ * TZ
KB = 256
UB = 128
UN = 2 * UB
ROW = NZ * KB
CUT = 768
NQ = 4
QR = UB // NQ

MESH = pl.DeviceIdType.MESH
BF = jnp.bfloat16
F32 = jnp.float32

root_half = 0.7071067811865476
inv_root_two_pi = 0.3989422804014327


def step(value, offset, size):
    return lax.rem(value + (offset + size), size)


def span(start, size):
    return pl.ds(pl.multiple_of(start, size), size)


def dot_nt(left, right):
    return lax.dot_general(
        left, right, (((1,), (1,)), ((), ())), preferred_element_type=F32
    )


def dot_nn(left, right):
    return lax.dot_general(
        left, right, (((1,), (0,)), ((), ())), preferred_element_type=F32
    )


def kernel(
    x_in, dy_in, wu_in, wd_in, ig_out, up_out, down_out, sq_out,
    wu, ws, xy, ww, wt, wsib, hid, gact, act_t, pre, pre_t, pre_sib,
    part, r1r, r1l, r2r, r2l, red, land,
    py, y1r, y1l, y2r, y2l, ty, z_r, z_l, fz, ox, nb,
    send, recv, local,
):
    dp, mp = lax.axis_index("dp"), lax.axis_index("mp")
    z, xh = lax.div(dp, 2), lax.rem(dp, 2)
    y, xl, c = lax.div(mp, 4), lax.rem(lax.div(mp, 2), 2), lax.rem(mp, 2)
    x = 2 * xh + xl

    def device(px, py_, pz, pc):
        return (pz * 2 + lax.div(px, 2), py_ * 4 + lax.rem(px, 2) * 2 + pc)

    def at_x(k):
        return device(step(x, k, NX), y, z, c)

    def at_y(k):
        return device(x, step(y, k, NY), z, c)

    def at_z(k):
        return device(x, y, step(z, k, NZ), c)

    sibling = device(x, y, z, 1 - c)

    started = []

    def push(src, dst, target):
        n = len(started)
        copy = pltpu.make_async_remote_copy(
            src_ref=src, dst_ref=dst, send_sem=send.at[n], recv_sem=recv.at[n],
            device_id=target, device_id_type=MESH,
        )
        copy.start()
        started.append(copy)
        return copy

    moved = []

    def move(src, dst):
        copy = pltpu.make_async_copy(src, dst, local.at[len(moved)])
        copy.start()
        moved.append(copy)
        return copy

    def land_all(copies):
        for copy in copies:
            copy.wait_recv()

    wu_own = move(wu_in, wu)
    wd_own = move(wd_in, ws.at[1])

    barrier = pltpu.get_barrier_semaphore()
    plane = [
        device(step(x, i, NX), step(y, j, NY), z, c)
        for i in range(NX) for j in range(NY) if i or j
    ]
    column = [
        device(x, y, step(z, k, NZ), pc)
        for k in range(NZ) for pc in (c, 1 - c) if k or pc is not c
    ]
    peers = plane + column
    for peer in peers:
        pl.semaphore_signal(barrier, inc=1, device_id=peer, device_id_type=MESH)

    wu_own.wait()

    @pl.loop(0, NZ)
    def _(t):
        at = span(t * UB, UB)
        ws[0, at, :] = wu[:, at].T

    wd_own.wait()
    pl.semaphore_wait(barrier, len(peers))

    first, rest = pl.ds(0, CUT), pl.ds(CUT, 4 * KB - CUT)

    def rows(pz):
        return span(pz * TZ, TZ)

    def half(pz, which):
        return span(pz * TZ + which * XT, XT)

    def cols(pz):
        return span(pz * KB, KB)

    def tok_place(a):
        return xy.at[c, y, span(z * TZ + xh * XT, XT), span((xl * 2 + a) * KB, KB)]

    tok, tok_own = [], []
    for k in (1, 3, 2):
        px = step(x, k, NX)
        for a, source in ((0, x_in), (1, dy_in)):
            tok.append(push(source.at[span(px * XT, XT), :], tok_place(a), at_x(k)))
    for a, source in ((0, x_in), (1, dy_in)):
        tok_own.append(move(source.at[span(x * XT, XT), :], tok_place(a)))

    w_place = ww.at[x, :, :, cols(z)]
    wz = {}

    def w_send(k):
        wz[k] = push(ws.at[:, span(step(z, k, NZ) * UB, UB), :], w_place, at_z(k))

    for k in (1, 7, 2, 6):
        w_send(k)
    w_own = move(ws.at[:, span(z * UB, UB), :], w_place)

    wx1, wx2 = {}, {}

    def w_hop1(k):
        if k:
            wz[k].wait_recv()
        piece = ww.at[x, :, :, cols(step(z, -k, NZ))]
        wx1[k] = [push(piece, piece, at_x(1)), push(piece, piece, at_x(-1))]

    def w_hop2(k):
        land_all(wx1[k])
        pz = cols(step(z, -k, NZ))
        right = ww.at[step(x, -1, NX), 0, :, pz]
        left = ww.at[step(x, 1, NX), 1, :, pz]
        wx2[k] = [push(right, right, at_x(1)), push(left, left, at_x(-1))]

    ya1, ya2, ca, cb, za, zb = {}, {}, {}, {}, {}, {}

    def ya_hop1(k):
        block = xy.at[c, y, rows(step(z, k, NZ)), first]
        ya1[k] = [push(block, block, at_y(1)), push(block, block, at_y(-1))]

    def ya_hop2(k):
        land_all(ya1[k])
        pz = step(z, k, NZ)
        right = xy.at[c, step(y, -1, NY), half(pz, 0), first]
        left = xy.at[c, step(y, 1, NY), half(pz, 1), first]
        ya2[k] = [push(right, right, at_y(1)), push(left, left, at_y(-1))]

    def ya_core(k):
        land_all(ya2[k])
        block = xy.at[c, :, rows(step(z, k, NZ)), first]
        ca[k] = push(block, block, sibling)

    def za_step(k):
        if k < 4:
            right = xy.at[c, y, rows(step(z, 1 - k, NZ)), first]
            left = xy.at[c, y, rows(step(z, k - 1, NZ)), first]
        else:
            right = xy.at[c, y, half(step(z, 1 - k, NZ), 0), first]
            left = xy.at[c, y, half(step(z, k - 1, NZ), 1), first]
        za[k] = [push(right, right, at_z(1)), push(left, left, at_z(-1))]

    def zb_step(k):
        if k < 4:
            right = xy.at[c, :, rows(step(z, 1 - k, NZ)), rest]
            left = xy.at[c, :, rows(step(z, k - 1, NZ)), rest]
        else:
            right = xy.at[c, :, half(step(z, 1 - k, NZ), 0), rest]
            left = xy.at[c, :, half(step(z, k - 1, NZ), 1), rest]
        zb[k] = [push(right, right, at_z(1)), push(left, left, at_z(-1))]

    def cb_core(k):
        block = xy.at[c, :, rows(step(z, k, NZ)), rest]
        cb[k] = push(block, block, sibling)

    def weight(which, pc, start):
        return ww[pl.ds(2 * pc, 2), which, :, span(start, KB)].reshape(UN, KB)

    def turn(k):
        land_all(wx2[k])
        pz = step(z, -k, NZ)

        @pl.loop(0, 2)
        def _(pc):
            for a in range(2):
                wt[a, pc, pz] = weight(a, pc, pz * KB).T

    pre_far = {}

    def hidden(ks):
        for k in ks:
            ca[k].wait_recv()
            cb[k].wait_recv()
        places = [rows(step(z, k, NZ)) for k in ks]
        size = TZ * len(ks)

        def operand(a, p):
            got = [
                jnp.concatenate(
                    [
                        xy[lax.div(p, NY), lax.rem(p, NY), at, pl.ds((2 * n + a) * KB, KB)]
                        for n in range(2)
                    ],
                    axis=1,
                )
                for at in places
            ]
            return got[0] if len(got) == 1 else jnp.concatenate(got, axis=0)

        hid[:size] = jnp.zeros((size, UN), F32)
        gact[:size] = jnp.zeros((size, UN), F32)

        @pl.loop(0, 2 * NY)
        def _(p):
            pair = pl.ds(2 * lax.rem(p, NY), 2)
            for a, total in ((0, hid), (1, gact)):
                right = wt[a, lax.div(p, NY), pair].reshape(2 * KB, UN)
                total[:size] += dot_nn(operand(a, p), right)

        for n, (k, at) in enumerate(zip(ks, places)):
            h = hid[n * TZ : (n + 1) * TZ]
            both = 0.5 * (1.0 + lax.erf(h * root_half))
            act = (h * both).astype(BF)
            slope = both + h * jnp.exp(-0.5 * h * h) * inv_root_two_pi
            grad = (gact[n * TZ : (n + 1) * TZ] * slope).astype(BF)
            pre[at, :] = grad
            pre_t[:, at] = grad.T
            act_t[:, at] = act.T
            pre_far[k] = push(pre.at[at, :], pre_sib.at[at, :], sibling)

    for copy in tok_own:
        copy.wait()
    land_all(tok)
    block = xy.at[c, y, rows(z), rest]
    yb1 = [push(block, block, at_y(1)), push(block, block, at_y(-1))]
    za_step(1)
    ya_hop1(0)
    w_own.wait()
    w_hop1(0)
    w_hop1(1)
    w_hop1(7)

    land_all(yb1)
    right = xy.at[c, step(y, -1, NY), half(z, 0), rest]
    left = xy.at[c, step(y, 1, NY), half(z, 1), rest]
    yb2 = [push(right, right, at_y(1)), push(left, left, at_y(-1))]
    w_hop1(2)
    w_hop1(6)
    land_all(yb2)
    zb_step(1)
    cb_core(0)
    ya_hop2(0)
    land_all(za[1])
    za_step(2)
    ya_hop1(1)
    ya_hop1(-1)
    w_hop2(0)
    w_hop2(1)
    w_hop2(7)
    ya_core(0)
    land_all(zb[1])
    zb_step(2)
    cb_core(1)
    cb_core(-1)
    w_hop2(2)
    w_hop2(6)
    land_all(za[2])
    za_step(3)
    w_send(3)
    w_send(5)
    w_send(4)
    ya_hop1(2)
    ya_hop1(-2)
    ya_hop2(1)
    ya_hop2(-1)
    for k in (0, 1, 7):
        turn(k)
    land_all(zb[2])
    cb_core(2)
    cb_core(-2)
    ya_core(1)
    ya_core(-1)
    land_all(za[3])
    za_step(4)
    zb_step(3)
    ya_hop1(3)
    ya_hop1(-3)
    turn(2)
    turn(6)
    ya_hop2(2)
    ya_hop2(-2)
    w_hop1(3)
    w_hop1(5)
    ya_core(2)
    ya_core(-2)
    w_hop1(4)
    land_all(za[4])
    ya_hop1(4)
    w_hop2(3)
    w_hop2(5)
    ya_hop2(3)
    ya_hop2(-3)
    w_hop2(4)
    land_all(zb[3])
    zb_step(4)
    cb_core(3)
    cb_core(-3)
    ya_core(3)
    ya_core(-3)
    for k in (3, 5, 4):
        turn(k)
    w_far = push(ww.at[pl.ds(2 * (1 - c), 2), 0, :, :], wsib, sibling)
    hidden((1, -1))
    ya_hop2(4)
    hidden((2, -2))
    land_all(zb[4])
    cb_core(4)
    ya_core(4)
    hidden((0, 3))
    hidden((-3, 4))

    def grad_parts(pc, a):
        left = pre_t if a == 0 else act_t

        @pl.loop(0, NZ)
        def _(q):
            right = xy[
                pc, lax.div(q, 2), :, span((2 * lax.rem(q, 2) + a) * KB, KB)
            ]
            out = dot_nn(left[...], right).astype(BF)
            part[2 * pc, a, :, cols(q)] = out[:UB]
            part[2 * pc + 1, a, :, cols(q)] = out[UB:]

    far, nxt, prv = step(x, 2, NX), step(x, 1, NX), step(x, -1, NX)
    x1, x2, gz, gz_own = {}, {}, [], []

    def piece(q):
        return pl.ds(q * QR, QR)

    def x_step1(q, a):
        src = part.at[far, a, piece(q), :]
        if a == 0:
            x1[q] = [push(src, r1r.at[q], at_x(1))]
        else:
            x1[q].append(push(src, r1l.at[q], at_x(-1)))

    def x_step2(q):
        land_all(x1[q])
        for px, a, got in ((nxt, 0, r1r), (prv, 1, r1l)):
            total = part[px, a, piece(q), :].astype(F32) + got[q].astype(F32)
            part[px, a, piece(q), :] = total.astype(BF)
        x2[q] = [
            push(part.at[nxt, :, piece(q), :], r2r.at[q], at_x(1)),
            push(part.at[prv, :, piece(q), :], r2l.at[q], at_x(-1)),
        ]

    def x_step3(q):
        land_all(x2[q])
        for a in range(2):
            total = (
                part[x, a, piece(q), :].astype(F32)
                + r2r[q, a].astype(F32)
                + r2l[q, a].astype(F32)
            )
            red[q, a] = total.astype(BF)
        place = land.at[:, span(z * UB + q * QR, QR), :]
        for k in (1, 7, 2, 6, 3, 5, 4):
            gz.append(push(red.at[q, :, :, cols(step(z, k, NZ))], place, at_z(k)))
        gz_own.append(move(red.at[q, :, :, cols(z)], place))

    half_tok = TOK // 2

    def ig_own(py_, h, side):
        at = pl.ds(side * half_tok, half_tok)
        start = (2 * py_ + h) * KB
        near = weight(0, c, start)
        other = wsib[:, :, span(start, KB)].reshape(UN, KB)
        return dot_nn(pre[at, :], near) + dot_nn(pre_sib[at, :], other)

    y1, y2 = {}, {}

    def y_step1(h):
        for side in range(2):
            at = pl.ds(side * half_tok, half_tok)
            py[0, h, at, :] = ig_own(step(y, 2, NY), h, side).astype(BF)
        y1[h] = [
            push(py.at[0, h, pl.ds(0, half_tok), :], y1r.at[h], at_y(1)),
            push(py.at[0, h, pl.ds(half_tok, half_tok), :], y1l.at[h], at_y(-1)),
        ]

    def y_step2(h):
        for k, slot, mine, got in ((1, 1, 0, y1r), (-1, 2, 1, y1l)):
            for side in range(2):
                at = pl.ds(side * half_tok, half_tok)
                total = ig_own(step(y, k, NY), h, side)
                if side == mine:
                    y1[h][mine].wait_recv()
                    total = total + got[h].astype(F32)
                py[slot, h, at, :] = total.astype(BF)
        y2[h] = [
            push(py.at[1, h], y2r.at[h], at_y(1)),
            push(py.at[2, h], y2l.at[h], at_y(-1)),
        ]

    def y_step3(h):
        land_all(y2[h])
        for side in range(2):
            at = pl.ds(side * half_tok, half_tok)
            total = (
                ig_own(y, h, side)
                + y2r[h, at, :].astype(F32)
                + y2l[h, at, :].astype(F32)
            )
            ty[h, at, :] = total.astype(BF)

    iz = {}

    def z_step(h, k):
        right, left = step(z, 5 - k, NZ), step(z, k - 5, NZ)
        if k == 1:
            iz[h, 1] = [
                push(ty.at[h, half(right, 0), :], z_r.at[h, 0, pl.ds(0, XT), :], at_z(1)),
                push(ty.at[h, half(left, 1), :], z_l.at[h, 0, pl.ds(XT, XT), :], at_z(-1)),
            ]
            return
        land_all(iz[h, k - 1])
        if k == 2:
            add_r, add_l = half(right, 0), half(left, 1)
            got_r, got_l = z_r[h, 0, :XT], z_l[h, 0, XT:]
        else:
            add_r, add_l = rows(right), rows(left)
            got_r, got_l = z_r[h, k - 2], z_l[h, k - 2]
        for at, got in ((add_r, got_r), (add_l, got_l)):
            ty[h, at, :] = (ty[h, at, :].astype(F32) + got.astype(F32)).astype(BF)
        iz[h, k] = [
            push(ty.at[h, rows(right), :], z_r.at[h, k - 1], at_z(1)),
            push(ty.at[h, rows(left), :], z_l.at[h, k - 1], at_z(-1)),
        ]

    def z_last(h):
        land_all(iz[h, 4])
        total = (
            ty[h, rows(z), :].astype(F32)
            + z_r[h, 3].astype(F32)
            + z_l[h, 3].astype(F32)
        )
        fz[h] = total.astype(BF)

    grad_parts(1 - xh, 0)
    x_step1(0, 0)
    x_step1(1, 0)
    for k in pre_far:
        pre_far[k].wait_recv()
    w_far.wait_recv()
    y_step1(0)
    grad_parts(1 - xh, 1)
    x_step1(0, 1)
    x_step1(1, 1)
    y_step1(1)
    grad_parts(xh, 0)
    grad_parts(xh, 1)
    x_step2(0)
    x_step1(2, 0)
    x_step1(2, 1)
    y_step2(0)
    x_step2(1)
    x_step1(3, 0)
    x_step1(3, 1)
    y_step2(1)
    x_step3(0)
    x_step2(2)
    x_step3(1)
    y_step3(0)
    z_step(0, 1)
    x_step2(3)
    z_step(0, 2)
    x_step3(2)
    z_step(0, 3)
    z_step(0, 4)
    y_step3(1)
    z_step(1, 1)
    x_step3(3)
    z_last(0)
    z_step(1, 2)
    z_step(1, 3)

    for copy in gz_own:
        copy.wait()
    land_all(gz)

    def square(t, total):
        for a in range(2):
            v = land[a, span(t * 64, 64), :].astype(F32)
            total = total + jnp.sum(v * v, axis=0, keepdims=True)
        return total

    squares = lax.fori_loop(0, 16, square, jnp.zeros((1, KB), F32))
    value = jnp.sum(squares, axis=1, keepdims=True)

    def exchange(stage, me, targets, value):
        nb[stage, me] = jnp.broadcast_to(value, (8, 128))
        return [push(nb.at[stage, me], nb.at[stage, me], t) for t in targets]

    def collect(stage, copies):
        land_all(copies)
        total = nb[stage, 0]
        for n in range(1, 16):
            total = total + nb[stage, n]
        return total[:1, :1]

    norm = exchange(0, 2 * z + c, column, value)
    z_step(1, 4)
    down_out[...] = land[1]
    value = collect(0, norm)
    norm = exchange(1, 4 * x + y, plane, value)
    z_last(1)

    def last(px):
        return fz.at[lax.rem(px, 2), span(lax.div(px, 2) * XT, XT), :]

    o_place = ox.at[span(x * XT, XT), :]
    o_far = [push(last(step(x, k, NX)), o_place, at_x(k)) for k in (1, 3, 2)]
    o_own = move(last(x), o_place)

    @pl.loop(0, NZ)
    def _(t):
        at = span(t * UB, UB)
        up_out[:, at] = land[0, at, :].T

    value = collect(1, norm)
    sq_out[...] = jnp.broadcast_to(value, (8, 128))
    o_own.wait()
    land_all(o_far)
    ig_out[...] = ox[...]

    for copy in started:
        copy.wait_send()


def on_device(inputs, cotangent, w_up, w_down):
    vmem = pl.BlockSpec(memory_space=pltpu.VMEM)
    hbm = pl.BlockSpec(memory_space=pl.ANY)
    ig, up, down, total = pl.pallas_call(
        kernel,
        out_shape=(
            jax.ShapeDtypeStruct((NX * XT, KB), BF),
            jax.ShapeDtypeStruct((KB, NZ * UB), BF),
            jax.ShapeDtypeStruct((NZ * UB, KB), BF),
            jax.ShapeDtypeStruct((8, 128), F32),
        ),
        in_specs=[hbm] * 4,
        out_specs=(vmem,) * 4,
        scratch_shapes=[
            pltpu.VMEM((KB, NZ * UB), BF),
            pltpu.VMEM((2, NZ * UB, KB), BF),
            pltpu.VMEM((2, NY, TOK, 4 * KB), BF),
            pltpu.VMEM((NX, 2, UB, ROW), BF),
            pltpu.VMEM((2, 2, NZ, KB, UN), BF),
            pltpu.VMEM((2, UB, ROW), BF),
            pltpu.VMEM((2 * TZ, UN), F32),
            pltpu.VMEM((2 * TZ, UN), F32),
            pltpu.VMEM((UN, TOK), BF),
            pltpu.VMEM((TOK, UN), BF),
            pltpu.VMEM((UN, TOK), BF),
            pltpu.VMEM((TOK, UN), BF),
            pltpu.VMEM((NX, 2, UB, ROW), BF),
            pltpu.VMEM((NQ, QR, ROW), BF),
            pltpu.VMEM((NQ, QR, ROW), BF),
            pltpu.VMEM((NQ, 2, QR, ROW), BF),
            pltpu.VMEM((NQ, 2, QR, ROW), BF),
            pltpu.VMEM((NQ, 2, QR, ROW), BF),
            pltpu.VMEM((2, NZ * UB, KB), BF),
            pltpu.VMEM((3, 2, TOK, KB), BF),
            pltpu.VMEM((2, TOK // 2, KB), BF),
            pltpu.VMEM((2, TOK // 2, KB), BF),
            pltpu.VMEM((2, TOK, KB), BF),
            pltpu.VMEM((2, TOK, KB), BF),
            pltpu.VMEM((2, TOK, KB), BF),
            pltpu.VMEM((2, 4, TZ, KB), BF),
            pltpu.VMEM((2, 4, TZ, KB), BF),
            pltpu.VMEM((2, TZ, KB), BF),
            pltpu.VMEM((NX * XT, KB), BF),
            pltpu.VMEM((2, 16, 8, 128), F32),
            pltpu.SemaphoreType.DMA((240,)),
            pltpu.SemaphoreType.DMA((240,)),
            pltpu.SemaphoreType.DMA((16,)),
        ],
        compiler_params=pltpu.CompilerParams(
            collective_id=0, has_side_effects=True, vmem_limit_bytes=60 * 2**20
        ),
        cost_estimate=pl.CostEstimate(
            flops=11_000_000_000, bytes_accessed=8_000_000, transcendentals=524288
        ),
    )(inputs, cotangent, w_up, w_down)
    mean_square = total[0, 0] / jnp.float32(2.0 * D * FF)
    scale = 1.0 / jnp.sqrt(mean_square)
    return ig, up.astype(F32) * scale, down.astype(F32) * scale, mean_square


def solution(mesh):
    placed = (P("dp", "mp"), P("dp", "mp"), P("dp", "mp"), P("mp", "dp"))
    return jax.shard_map(
        on_device,
        mesh=mesh,
        in_specs=placed,
        out_specs=(P("dp", "mp"), P("dp", "mp"), P("mp", "dp"), P()),
        check_vma=False,
    )
```

time: 199 us -> 166 us (0.83)
  Pallas kernels: 186 us -> 158 us
  local copies, waits for them, and re-layouts: 4.19 us -> 1.85 us
    pallas_call x1, Pallas kernels: 186 us -> 158 us  [on_device(): pl.pallas_call(kernel, out_shape=(jax.ShapeDtypeStruct((NX * XT, KB), BF)...]
    unnamed x9 -> x5, local copies, waits for them, and re-layouts: 3.01 us -> 0.66 us
where the time goes in v2:
time: 166 us
  Pallas kernels  158 us (95%)
  other arithmetic  3.23 us (2%)
  between operations  2.47 us (1%)
  local copies, waits for them, and re-layouts  1.85 us (1%)
    pallas_call x1, Pallas kernels, on_device(): pl.pallas_call(kernel, out_shape=(jax.ShapeDtypeStruct((NX * XT, KB), BF)...  158 us

profile of v2, /device:TPU:1, one launch (start us, length us, event | category | flops | bytes accessed | tf_op | source)
XLA Modules:
  0.0 165.7 jit_solution(7739050561671059761)
XLA Ops:
  0.6 158.2 %shard_map.75 = (bf16[256,256]{1,0:T(8,128)(2,1)}, bf16[256,1024]{1,0:T(8,128)(2,1)}, bf16[1024,256]{1,0:T(8,128)(2,1)}, f32[8,128]{1,0:T(8,128)}) custom-call(bf16[256,256]{1,0:T(8,128)(2,1)} %x_in.1, bf16[256,256]{1,0:T(8,128)(2,1)} %dy_in.1, bf16[256,1024]{1,0:T(8,128)(2,1)} %wu_in.1, bf16[1024,256]{1,0:T(8,128)(2,1)} %wd_in.1), custom_call_target="tpu_custom_call" | custom-call | flops 11000000512 | bytes 8000000 | tf_op jit(solution)/shard_map/pallas_call | solution.py:581
  158.8 1.2 slice.3
  160.7 0.0 copy-start
  160.7 2.2 %convert_multiply_fusion.1 = f32[256,1024]{1,0:T(8,128)} fusion(bf16[256,1024]{1,0:T(8,128)(2,1)} %get-tuple-element.9, f32[]{:T(128)S(6)} %sqrt.3), kind=kLoop, calls=%fused_computation.1 | loop fusion | flops 524288 | bytes 1572868 | tf_op jit(solution)/shard_map/mul | solution.py:635
  162.9 0.0 copy-done
  162.9 0.0 copy-start.1
  162.9 1.0 convert_multiply_fusion
  163.9 0.0 copy-done.1
  163.9 0.7 copy.9
Async XLA Ops:
  160.7 2.2 %copy-start = (bf16[1024,256]{1,0:T(8,128)(2,1)S(1)}, bf16[1024,256]{1,0:T(8,128)(2,1)}, u32[]{:S(2)}) copy-start(bf16[1024,256]{1,0:T(8,128)(2,1)} %get-tuple-element.11) | copy-start | bytes 1572868
  162.9 1.0 copy-start.1

commit v3 on v2

--- a/solution.py
+++ b/solution.py
@@ -17,8 +17,7 @@
 UN = 2 * UB
 ROW = NZ * KB
 CUT = 768
-NQ = 4
-QR = UB // NQ
+PIECES = (0, 16, 32, 64, 96, 112, 128)
 
 MESH = pl.DeviceIdType.MESH
 BF = jnp.bfloat16
@@ -114,14 +113,6 @@
     for peer in peers:
         pl.semaphore_signal(barrier, inc=1, device_id=peer, device_id_type=MESH)
 
-    wu_own.wait()
-
-    @pl.loop(0, NZ)
-    def _(t):
-        at = span(t * UB, UB)
-        ws[0, at, :] = wu[:, at].T
-
-    wd_own.wait()
     pl.semaphore_wait(barrier, len(peers))
 
     first, rest = pl.ds(0, CUT), pl.ds(CUT, 4 * KB - CUT)
@@ -146,26 +137,40 @@
     for a, source in ((0, x_in), (1, dy_in)):
         tok_own.append(move(source.at[span(x * XT, XT), :], tok_place(a)))
 
+    wu_own.wait()
+
+    @pl.loop(0, NZ)
+    def _(t):
+        at = span(t * UB, UB)
+        ws[0, at, :] = wu[:, at].T
+
+    wd_own.wait()
     w_place = ww.at[x, :, :, cols(z)]
     wz = {}
 
     def w_send(k):
         wz[k] = push(ws.at[:, span(step(z, k, NZ) * UB, UB), :], w_place, at_z(k))
 
-    for k in (1, 7, 2, 6):
-        w_send(k)
+    w_send(1)
+    w_send(7)
     w_own = move(ws.at[:, span(z * UB, UB), :], w_place)
 
     wx1, wx2 = {}, {}
+
+    direct = (3, 5, 4)
 
     def w_hop1(k):
         if k:
             wz[k].wait_recv()
         piece = ww.at[x, :, :, cols(step(z, -k, NZ))]
         wx1[k] = [push(piece, piece, at_x(1)), push(piece, piece, at_x(-1))]
+        if k in direct:
+            wx2[k] = [push(piece, piece, at_x(2))]
 
     def w_hop2(k):
         land_all(wx1[k])
+        if k in direct:
+            return
         pz = cols(step(z, -k, NZ))
         right = ww.at[step(x, -1, NX), 0, :, pz]
         left = ww.at[step(x, 1, NX), 1, :, pz]
@@ -256,15 +261,16 @@
                 total[:size] += dot_nn(operand(a, p), right)
 
         for n, (k, at) in enumerate(zip(ks, places)):
+            pz = step(z, k, NZ)
             h = hid[n * TZ : (n + 1) * TZ]
             both = 0.5 * (1.0 + lax.erf(h * root_half))
             act = (h * both).astype(BF)
             slope = both + h * jnp.exp(-0.5 * h * h) * inv_root_two_pi
             grad = (gact[n * TZ : (n + 1) * TZ] * slope).astype(BF)
-            pre[at, :] = grad
+            pre[pz] = grad
             pre_t[:, at] = grad.T
             act_t[:, at] = act.T
-            pre_far[k] = push(pre.at[at, :], pre_sib.at[at, :], sibling)
+            pre_far[k] = push(pre.at[pz], pre_sib.at[pz], sibling)
 
     for copy in tok_own:
         copy.wait()
@@ -273,6 +279,8 @@
     yb1 = [push(block, block, at_y(1)), push(block, block, at_y(-1))]
     za_step(1)
     ya_hop1(0)
+    w_send(2)
+    w_send(6)
     w_own.wait()
     w_hop1(0)
     w_hop1(1)
@@ -282,19 +290,27 @@
     right = xy.at[c, step(y, -1, NY), half(z, 0), rest]
     left = xy.at[c, step(y, 1, NY), half(z, 1), rest]
     yb2 = [push(right, right, at_y(1)), push(left, left, at_y(-1))]
-    w_hop1(2)
-    w_hop1(6)
-    land_all(yb2)
-    zb_step(1)
-    cb_core(0)
-    ya_hop2(0)
     land_all(za[1])
     za_step(2)
     ya_hop1(1)
     ya_hop1(-1)
+    ya_hop2(0)
+    land_all(yb2)
+    zb_step(1)
+    cb_core(0)
+    w_hop1(2)
+    w_hop1(6)
     w_hop2(0)
     w_hop2(1)
     w_hop2(7)
+    land_all(za[2])
+    za_step(3)
+    ya_hop1(2)
+    ya_hop1(-2)
+    w_send(3)
+    w_send(5)
+    ya_hop2(1)
+    ya_hop2(-1)
     ya_core(0)
     land_all(zb[1])
     zb_step(2)
@@ -302,60 +318,52 @@
     cb_core(-1)
     w_hop2(2)
     w_hop2(6)
-    land_all(za[2])
-    za_step(3)
-    w_send(3)
-    w_send(5)
-    w_send(4)
-    ya_hop1(2)
-    ya_hop1(-2)
-    ya_hop2(1)
-    ya_hop2(-1)
-    for k in (0, 1, 7):
-        turn(k)
-    land_all(zb[2])
-    cb_core(2)
-    cb_core(-2)
-    ya_core(1)
-    ya_core(-1)
+    turn(0)
+    turn(1)
+    turn(7)
     land_all(za[3])
     za_step(4)
-    zb_step(3)
+    w_send(4)
     ya_hop1(3)
     ya_hop1(-3)
     turn(2)
     turn(6)
     ya_hop2(2)
     ya_hop2(-2)
+    ya_core(1)
+    ya_core(-1)
     w_hop1(3)
     w_hop1(5)
+    land_all(zb[2])
+    zb_step(3)
+    cb_core(2)
+    cb_core(-2)
+    land_all(za[4])
+    ya_hop1(4)
+    ya_hop2(3)
+    ya_hop2(-3)
     ya_core(2)
     ya_core(-2)
-    w_hop1(4)
-    land_all(za[4])
-    ya_hop1(4)
     w_hop2(3)
     w_hop2(5)
-    ya_hop2(3)
-    ya_hop2(-3)
-    w_hop2(4)
+    turn(3)
+    turn(5)
+    w_hop1(4)
     land_all(zb[3])
     zb_step(4)
     cb_core(3)
     cb_core(-3)
+    ya_hop2(4)
     ya_core(3)
     ya_core(-3)
-    for k in (3, 5, 4):
-        turn(k)
+    w_hop2(4)
+    turn(4)
     w_far = push(ww.at[pl.ds(2 * (1 - c), 2), 0, :, :], wsib, sibling)
-    hidden((1, -1))
-    ya_hop2(4)
-    hidden((2, -2))
+    ya_core(4)
+    hidden((0, 1, -1, 2, -2))
     land_all(zb[4])
     cb_core(4)
-    ya_core(4)
-    hidden((0, 3))
-    hidden((-3, 4))
+    hidden((3, -3, 4))
 
     def grad_parts(pc, a):
         left = pre_t if a == 0 else act_t
@@ -370,170 +378,204 @@
             part[2 * pc + 1, a, :, cols(q)] = out[UB:]
 
     far, nxt, prv = step(x, 2, NX), step(x, 1, NX), step(x, -1, NX)
-    x1, x2, gz, gz_own = {}, {}, [], []
+    x1, x2, gz, gz_own = {}, {}, {}, {}
 
     def piece(q):
-        return pl.ds(q * QR, QR)
+        return pl.ds(PIECES[q], PIECES[q + 1] - PIECES[q])
 
     def x_step1(q, a):
         src = part.at[far, a, piece(q), :]
         if a == 0:
-            x1[q] = [push(src, r1r.at[q], at_x(1))]
+            x1[q] = [push(src, r1r.at[piece(q), :], at_x(1))]
         else:
-            x1[q].append(push(src, r1l.at[q], at_x(-1)))
+            x1[q].append(push(src, r1l.at[piece(q), :], at_x(-1)))
 
     def x_step2(q):
         land_all(x1[q])
+        at = piece(q)
         for px, a, got in ((nxt, 0, r1r), (prv, 1, r1l)):
-            total = part[px, a, piece(q), :].astype(F32) + got[q].astype(F32)
-            part[px, a, piece(q), :] = total.astype(BF)
+            total = part[px, a, at, :].astype(F32) + got[at, :].astype(F32)
+            part[px, a, at, :] = total.astype(BF)
         x2[q] = [
-            push(part.at[nxt, :, piece(q), :], r2r.at[q], at_x(1)),
-            push(part.at[prv, :, piece(q), :], r2l.at[q], at_x(-1)),
+            push(part.at[nxt, :, at, :], r2r.at[:, at, :], at_x(1)),
+            push(part.at[prv, :, at, :], r2l.at[:, at, :], at_x(-1)),
         ]
 
     def x_step3(q):
         land_all(x2[q])
+        at = piece(q)
         for a in range(2):
             total = (
-                part[x, a, piece(q), :].astype(F32)
-                + r2r[q, a].astype(F32)
-                + r2l[q, a].astype(F32)
+                part[x, a, at, :].astype(F32)
+                + r2r[a, at, :].astype(F32)
+                + r2l[a, at, :].astype(F32)
             )
-            red[q, a] = total.astype(BF)
-        place = land.at[:, span(z * UB + q * QR, QR), :]
-        for k in (1, 7, 2, 6, 3, 5, 4):
-            gz.append(push(red.at[q, :, :, cols(step(z, k, NZ))], place, at_z(k)))
-        gz_own.append(move(red.at[q, :, :, cols(z)], place))
-
-    half_tok = TOK // 2
-
-    def ig_own(py_, h, side):
-        at = pl.ds(side * half_tok, half_tok)
-        start = (2 * py_ + h) * KB
+            red[a, at, :] = total.astype(BF)
+        place = land.at[:, pl.ds(pl.multiple_of(z * UB + PIECES[q], 16), at.size), :]
+        gz[q] = [
+            push(red.at[:, at, cols(step(z, k, NZ))], place, at_z(k))
+            for k in (1, 7, 2, 6, 3, 5, 4)
+        ]
+        gz_own[q] = move(red.at[:, at, cols(z)], place)
+
+    def squares(q, total):
+        gz_own[q].wait()
+        land_all(gz[q])
+        at = piece(q)
+        for a in range(2):
+            for n in range(NZ):
+                v = land[a, pl.ds(n * UB + at.start, at.size), :].astype(F32)
+                total = total + jnp.sum(v * v, axis=0, keepdims=True)
+        return total
+
+    pieces = (2, 1, 3, 0)
+    size = NZ * XT
+
+    def ig_own(py_, j):
+        px = step(x, pieces[j], NX)
+        tokens = span(lax.div(px, 2) * XT, XT)
+        start = (2 * py_ + lax.rem(px, 2)) * KB
         near = weight(0, c, start)
         other = wsib[:, :, span(start, KB)].reshape(UN, KB)
-        return dot_nn(pre[at, :], near) + dot_nn(pre_sib[at, :], other)
+        return dot_nn(pre[:, tokens, :].reshape(size, UN), near) + dot_nn(
+            pre_sib[:, tokens, :].reshape(size, UN), other
+        )
 
     y1, y2 = {}, {}
-
-    def y_step1(h):
-        for side in range(2):
-            at = pl.ds(side * half_tok, half_tok)
-            py[0, h, at, :] = ig_own(step(y, 2, NY), h, side).astype(BF)
-        y1[h] = [
-            push(py.at[0, h, pl.ds(0, half_tok), :], y1r.at[h], at_y(1)),
-            push(py.at[0, h, pl.ds(half_tok, half_tok), :], y1l.at[h], at_y(-1)),
+    low, high = pl.ds(0, size // 2), pl.ds(size // 2, size // 2)
+
+    def y_step1(j):
+        py[0, j] = ig_own(step(y, 2, NY), j).astype(BF)
+        y1[j] = [
+            push(py.at[0, j, low, :], y1r.at[j], at_y(1)),
+            push(py.at[0, j, high, :], y1l.at[j], at_y(-1)),
         ]
 
-    def y_step2(h):
-        for k, slot, mine, got in ((1, 1, 0, y1r), (-1, 2, 1, y1l)):
-            for side in range(2):
-                at = pl.ds(side * half_tok, half_tok)
-                total = ig_own(step(y, k, NY), h, side)
-                if side == mine:
-                    y1[h][mine].wait_recv()
-                    total = total + got[h].astype(F32)
-                py[slot, h, at, :] = total.astype(BF)
-        y2[h] = [
-            push(py.at[1, h], y2r.at[h], at_y(1)),
-            push(py.at[2, h], y2l.at[h], at_y(-1)),
-        ]
-
-    def y_step3(h):
-        land_all(y2[h])
-        for side in range(2):
-            at = pl.ds(side * half_tok, half_tok)
-            total = (
-                ig_own(y, h, side)
-                + y2r[h, at, :].astype(F32)
-                + y2l[h, at, :].astype(F32)
-            )
-            ty[h, at, :] = total.astype(BF)
+    def y_step2(j):
+        total = ig_own(step(y, 1, NY), j)
+        y1[j][0].wait_recv()
+        py[1, j, low, :] = (total[: size // 2] + y1r[j].astype(F32)).astype(BF)
+        py[1, j, high, :] = total[size // 2 :].astype(BF)
+        right = push(py.at[1, j], y2r.at[j], at_y(1))
+        total = ig_own(step(y, -1, NY), j)
+        y1[j][1].wait_recv()
+        py[2, j, low, :] = total[: size // 2].astype(BF)
+        py[2, j, high, :] = (total[size // 2 :] + y1l[j].astype(F32)).astype(BF)
+        y2[j] = [right, push(py.at[2, j], y2l.at[j], at_y(-1))]
+
+    def y_step3(j):
+        total = ig_own(y, j)
+        land_all(y2[j])
+        ty[j] = (total + y2r[j].astype(F32) + y2l[j].astype(F32)).astype(BF)
 
     iz = {}
-
-    def z_step(h, k):
+    XH = XT // 2
+
+    def band(pz):
+        return span(pz * XT, XT)
+
+    def part_band(pz, which):
+        return span(pz * XT + which * XH, XH)
+
+    def z_step(j, k):
         right, left = step(z, 5 - k, NZ), step(z, k - 5, NZ)
         if k == 1:
-            iz[h, 1] = [
-                push(ty.at[h, half(right, 0), :], z_r.at[h, 0, pl.ds(0, XT), :], at_z(1)),
-                push(ty.at[h, half(left, 1), :], z_l.at[h, 0, pl.ds(XT, XT), :], at_z(-1)),
+            iz[j, 1] = [
+                push(ty.at[j, part_band(right, 0), :], z_r.at[j, 0, pl.ds(0, XH), :], at_z(1)),
+                push(ty.at[j, part_band(left, 1), :], z_l.at[j, 0, pl.ds(XH, XH), :], at_z(-1)),
             ]
             return
-        land_all(iz[h, k - 1])
+        land_all(iz[j, k - 1])
         if k == 2:
-            add_r, add_l = half(right, 0), half(left, 1)
-            got_r, got_l = z_r[h, 0, :XT], z_l[h, 0, XT:]
+            add_r, add_l = part_band(right, 0), part_band(left, 1)
+            got_r, got_l = z_r[j, 0, :XH], z_l[j, 0, XH:]
         else:
-            add_r, add_l = rows(right), rows(left)
-            got_r, got_l = z_r[h, k - 2], z_l[h, k - 2]
+            add_r, add_l = band(right), band(left)
+            got_r, got_l = z_r[j, k - 2], z_l[j, k - 2]
         for at, got in ((add_r, got_r), (add_l, got_l)):
-            ty[h, at, :] = (ty[h, at, :].astype(F32) + got.astype(F32)).astype(BF)
-        iz[h, k] = [
-            push(ty.at[h, rows(right), :], z_r.at[h, k - 1], at_z(1)),
-            push(ty.at[h, rows(left), :], z_l.at[h, k - 1], at_z(-1)),
+            ty[j, at, :] = (ty[j, at, :].astype(F32) + got.astype(F32)).astype(BF)
+        iz[j, k] = [
+            push(ty.at[j, band(right), :], z_r.at[j, k - 1], at_z(1)),
+            push(ty.at[j, band(left), :], z_l.at[j, k - 1], at_z(-1)),
         ]
 
-    def z_last(h):
-        land_all(iz[h, 4])
+    far_out = []
+
+    def z_last(j):
+        land_all(iz[j, 4])
         total = (
-            ty[h, rows(z), :].astype(F32)
-            + z_r[h, 3].astype(F32)
-            + z_l[h, 3].astype(F32)
-        )
-        fz[h] = total.astype(BF)
+            ty[j, band(z), :].astype(F32)
+            + z_r[j, 3].astype(F32)
+            + z_l[j, 3].astype(F32)
+        ).astype(BF)
+        if pieces[j]:
+            fz[j] = total
+            far_out.append(
+                push(fz.at[j], ox.at[span(x * XT, XT), :], at_x(pieces[j]))
+            )
+        else:
+            ox[span(x * XT, XT), :] = total
 
     grad_parts(1 - xh, 0)
-    x_step1(0, 0)
-    x_step1(1, 0)
+    for q in range(4):
+        x_step1(q, 0)
     for k in pre_far:
         pre_far[k].wait_recv()
     w_far.wait_recv()
     y_step1(0)
+    y_step1(1)
     grad_parts(1 - xh, 1)
-    x_step1(0, 1)
-    x_step1(1, 1)
-    y_step1(1)
+    for q in range(4):
+        x_step1(q, 1)
+    y_step1(2)
     grad_parts(xh, 0)
     grad_parts(xh, 1)
     x_step2(0)
-    x_step1(2, 0)
-    x_step1(2, 1)
     y_step2(0)
     x_step2(1)
-    x_step1(3, 0)
-    x_step1(3, 1)
+    y_step1(3)
     y_step2(1)
+    x_step2(2)
+    for q in (4, 5):
+        x_step1(q, 0)
+        x_step1(q, 1)
     x_step3(0)
-    x_step2(2)
+    y_step2(2)
     x_step3(1)
     y_step3(0)
+    x_step2(3)
+    y_step2(3)
+    x_step3(2)
+    y_step3(1)
     z_step(0, 1)
-    x_step2(3)
+    z_step(1, 1)
+    x_step2(4)
+    x_step2(5)
+    y_step3(2)
     z_step(0, 2)
-    x_step3(2)
+    z_step(1, 2)
+    x_step3(3)
+    total = squares(0, jnp.zeros((1, KB), F32))
+    total = squares(1, total)
+    y_step3(3)
+    z_step(2, 1)
+    z_step(3, 1)
     z_step(0, 3)
+    z_step(1, 3)
+    x_step3(4)
+    x_step3(5)
+    total = squares(2, total)
+    z_step(2, 2)
+    z_step(3, 2)
     z_step(0, 4)
-    y_step3(1)
-    z_step(1, 1)
-    x_step3(3)
-    z_last(0)
-    z_step(1, 2)
-    z_step(1, 3)
-
-    for copy in gz_own:
-        copy.wait()
-    land_all(gz)
-
-    def square(t, total):
-        for a in range(2):
-            v = land[a, span(t * 64, 64), :].astype(F32)
-            total = total + jnp.sum(v * v, axis=0, keepdims=True)
-        return total
-
-    squares = lax.fori_loop(0, 16, square, jnp.zeros((1, KB), F32))
-    value = jnp.sum(squares, axis=1, keepdims=True)
+    z_step(1, 4)
+    total = squares(3, total)
+    z_step(2, 3)
+    z_step(3, 3)
+    total = squares(4, total)
+
+    total = squares(5, total)
+    value = jnp.sum(total, axis=1, keepdims=True)
 
     def exchange(stage, me, targets, value):
         nb[stage, me] = jnp.broadcast_to(value, (8, 128))
@@ -547,29 +589,25 @@
         return total[:1, :1]
 
     norm = exchange(0, 2 * z + c, column, value)
-    z_step(1, 4)
-    down_out[...] = land[1]
+    z_last(0)
+    z_last(1)
+    z_step(2, 4)
+    z_step(3, 4)
     value = collect(0, norm)
     norm = exchange(1, 4 * x + y, plane, value)
-    z_last(1)
-
-    def last(px):
-        return fz.at[lax.rem(px, 2), span(lax.div(px, 2) * XT, XT), :]
-
-    o_place = ox.at[span(x * XT, XT), :]
-    o_far = [push(last(step(x, k, NX)), o_place, at_x(k)) for k in (1, 3, 2)]
-    o_own = move(last(x), o_place)
+    down_out[...] = land[1]
+    z_last(2)
 
     @pl.loop(0, NZ)
     def _(t):
         at = span(t * UB, UB)
         up_out[:, at] = land[0, at, :].T
 
+    z_last(3)
+    land_all(far_out)
+    ig_out[...] = ox[...]
     value = collect(1, norm)
-    sq_out[...] = jnp.broadcast_to(value, (8, 128))
-    o_own.wait()
-    land_all(o_far)
-    ig_out[...] = ox[...]
+    sq_out[0, 0] = jnp.max(value)
 
     for copy in started:
         copy.wait_send()
@@ -584,10 +622,10 @@
             jax.ShapeDtypeStruct((NX * XT, KB), BF),
             jax.ShapeDtypeStruct((KB, NZ * UB), BF),
             jax.ShapeDtypeStruct((NZ * UB, KB), BF),
-            jax.ShapeDtypeStruct((8, 128), F32),
+            jax.ShapeDtypeStruct((1, 1), F32),
         ),
         in_specs=[hbm] * 4,
-        out_specs=(vmem,) * 4,
+        out_specs=(vmem, vmem, vmem, pl.BlockSpec(memory_space=pltpu.SMEM)),
         scratch_shapes=[
             pltpu.VMEM((KB, NZ * UB), BF),
             pltpu.VMEM((2, NZ * UB, KB), BF),
@@ -595,33 +633,33 @@
             pltpu.VMEM((NX, 2, UB, ROW), BF),
             pltpu.VMEM((2, 2, NZ, KB, UN), BF),
             pltpu.VMEM((2, UB, ROW), BF),
-            pltpu.VMEM((2 * TZ, UN), F32),
-            pltpu.VMEM((2 * TZ, UN), F32),
+            pltpu.VMEM((5 * TZ, UN), F32),
+            pltpu.VMEM((5 * TZ, UN), F32),
             pltpu.VMEM((UN, TOK), BF),
-            pltpu.VMEM((TOK, UN), BF),
+            pltpu.VMEM((NZ, TZ, UN), BF),
             pltpu.VMEM((UN, TOK), BF),
-            pltpu.VMEM((TOK, UN), BF),
+            pltpu.VMEM((NZ, TZ, UN), BF),
             pltpu.VMEM((NX, 2, UB, ROW), BF),
-            pltpu.VMEM((NQ, QR, ROW), BF),
-            pltpu.VMEM((NQ, QR, ROW), BF),
-            pltpu.VMEM((NQ, 2, QR, ROW), BF),
-            pltpu.VMEM((NQ, 2, QR, ROW), BF),
-            pltpu.VMEM((NQ, 2, QR, ROW), BF),
+            pltpu.VMEM((UB, ROW), BF),
+            pltpu.VMEM((UB, ROW), BF),
+            pltpu.VMEM((2, UB, ROW), BF),
+            pltpu.VMEM((2, UB, ROW), BF),
+            pltpu.VMEM((2, UB, ROW), BF),
             pltpu.VMEM((2, NZ * UB, KB), BF),
-            pltpu.VMEM((3, 2, TOK, KB), BF),
-            pltpu.VMEM((2, TOK // 2, KB), BF),
-            pltpu.VMEM((2, TOK // 2, KB), BF),
-            pltpu.VMEM((2, TOK, KB), BF),
-            pltpu.VMEM((2, TOK, KB), BF),
-            pltpu.VMEM((2, TOK, KB), BF),
-            pltpu.VMEM((2, 4, TZ, KB), BF),
-            pltpu.VMEM((2, 4, TZ, KB), BF),
-            pltpu.VMEM((2, TZ, KB), BF),
+            pltpu.VMEM((3, 4, NZ * XT, KB), BF),
+            pltpu.VMEM((4, NZ * XT // 2, KB), BF),
+            pltpu.VMEM((4, NZ * XT // 2, KB), BF),
+            pltpu.VMEM((4, NZ * XT, KB), BF),
+            pltpu.VMEM((4, NZ * XT, KB), BF),
+            pltpu.VMEM((4, NZ * XT, KB), BF),
+            pltpu.VMEM((4, 4, XT, KB), BF),
+            pltpu.VMEM((4, 4, XT, KB), BF),
+            pltpu.VMEM((4, XT, KB), BF),
             pltpu.VMEM((NX * XT, KB), BF),
             pltpu.VMEM((2, 16, 8, 128), F32),
-            pltpu.SemaphoreType.DMA((240,)),
-            pltpu.SemaphoreType.DMA((240,)),
-            pltpu.SemaphoreType.DMA((16,)),
+            pltpu.SemaphoreType.DMA((304,)),
+            pltpu.SemaphoreType.DMA((304,)),
+            pltpu.SemaphoreType.DMA((24,)),
         ],
         compiler_params=pltpu.CompilerParams(
             collective_id=0, has_side_effects=True, vmem_limit_bytes=60 * 2**20

time: 166 us -> 161 us (0.970)
  Pallas kernels: 158 us -> 155 us
    pallas_call x1, Pallas kernels: 158 us -> 155 us  [on_device(): pl.pallas_call(kernel, out_shape=(jax.ShapeDtypeStruct((NX * XT, KB), BF)...]
where the time goes in v3:
time: 161 us
  Pallas kernels  155 us (96%)
  other arithmetic  3.23 us (2%)
  between operations  2.45 us (2%)
    pallas_call x1, Pallas kernels, on_device(): pl.pallas_call(kernel, out_shape=(jax.ShapeDtypeStruct((NX * XT, KB), BF)...  155 us
    mul x2, other arithmetic, on_device(): return (ig, up.astype(F32) * scale, down.astype(F32) * scale, mean_square)  3.23 us

profile of v3, /device:TPU:1, one launch (start us, length us, event | category | flops | bytes accessed | tf_op | source)
XLA Modules:
  0.0 161.0 jit_solution(5471744213158779351)
XLA Ops:
  0.6 154.6 %shard_map.75 = (bf16[256,256]{1,0:T(8,128)(2,1)}, bf16[256,1024]{1,0:T(8,128)(2,1)}, bf16[1024,256]{1,0:T(8,128)(2,1)}, f32[1,1]{1,0:T(1,128)}) custom-call(bf16[256,256]{1,0:T(8,128)(2,1)} %x_in.1, bf16[256,256]{1,0:T(8,128)(2,1)} %dy_in.1, bf16[256,1024]{1,0:T(8,128)(2,1)} %wu_in.1, bf16[1024,256]{1,0:T(8,128)(2,1)} %wd_in.1), custom_call_target="tpu_custom_call" | custom-call | flops 11000000512 | bytes 8000000 | tf_op jit(solution)/shard_map/pallas_call | solution.py:619
  155.9 0.0 copy-start
  155.9 2.2 %convert_multiply_fusion.1 = f32[256,1024]{1,0:T(8,128)} fusion(bf16[256,1024]{1,0:T(8,128)(2,1)} %get-tuple-element.9, f32[]{:T(128)S(6)} %sqrt.3), kind=kLoop, calls=%fused_computation.1 | loop fusion | flops 524288 | bytes 1572868 | tf_op jit(solution)/shard_map/mul | solution.py:673
  158.1 0.0 copy-done
  158.1 0.0 copy-start.1
  158.1 1.0 convert_multiply_fusion
  159.2 0.0 copy-done.1
  159.2 0.7 copy.9
Async XLA Ops:
  155.9 2.2 %copy-start = (bf16[1024,256]{1,0:T(8,128)(2,1)S(1)}, bf16[1024,256]{1,0:T(8,128)(2,1)}, u32[]{:S(2)}) copy-start(bf16[1024,256]{1,0:T(8,128)(2,1)} %get-tuple-element.11) | copy-start | bytes 1572868
  158.1 1.0 copy-start.1

commit v4 on v3

--- a/solution.py
+++ b/solution.py
@@ -48,10 +48,10 @@
 
 
 def kernel(
-    x_in, dy_in, wu_in, wd_in, ig_out, up_out, down_out, sq_out,
+    x_in, dy_in, wu_in, wd_in, ig_out, up_out, down_out, sq_out, scale_out,
     wu, ws, xy, ww, wt, wsib, hid, gact, act_t, pre, pre_t, pre_sib,
     part, r1r, r1l, r2r, r2l, red, land,
-    py, y1r, y1l, y2r, y2l, ty, z_r, z_l, fz, ox, nb,
+    py, y1r, y1l, y2r, y2l, ty, z_r, z_l, fz, ox, up_t, squares, nb,
     send, recv, local,
 ):
     dp, mp = lax.axis_index("dp"), lax.axis_index("mp")
@@ -109,7 +109,12 @@
         device(x, y, step(z, k, NZ), pc)
         for k in range(NZ) for pc in (c, 1 - c) if k or pc is not c
     ]
-    peers = plane + column
+    peers = (
+        [at_x(k) for k in range(1, NX)]
+        + [at_y(k) for k in range(1, NY)]
+        + [at_z(k) for k in range(1, NZ)]
+        + [sibling]
+    )
     for peer in peers:
         pl.semaphore_signal(barrier, inc=1, device_id=peer, device_id_type=MESH)
 
@@ -230,18 +235,22 @@
 
     pre_far = {}
 
-    def hidden(ks):
+    def land_blocks(ks):
         for k in ks:
             ca[k].wait_recv()
             cb[k].wait_recv()
+
+    late = lax.div(step(z, 4, NZ), 2)
+
+    def hidden_sums(ks, chunks):
         places = [rows(step(z, k, NZ)) for k in ks]
         size = TZ * len(ks)
 
-        def operand(a, p):
+        def operand(a, pc, py_):
             got = [
                 jnp.concatenate(
                     [
-                        xy[lax.div(p, NY), lax.rem(p, NY), at, pl.ds((2 * n + a) * KB, KB)]
+                        xy[pc, py_, at, pl.ds((2 * n + a) * KB, KB)]
                         for n in range(2)
                     ],
                     axis=1,
@@ -250,16 +259,20 @@
             ]
             return got[0] if len(got) == 1 else jnp.concatenate(got, axis=0)
 
-        hid[:size] = jnp.zeros((size, UN), F32)
-        gact[:size] = jnp.zeros((size, UN), F32)
-
-        @pl.loop(0, 2 * NY)
+        if chunks[0] == 1:
+            hid[:size] = jnp.zeros((size, UN), F32)
+            gact[:size] = jnp.zeros((size, UN), F32)
+
+        @pl.loop(0, 2 * len(chunks))
         def _(p):
-            pair = pl.ds(2 * lax.rem(p, NY), 2)
+            pc = lax.rem(p, 2)
+            py_ = lax.rem(late + chunks[0] + lax.div(p, 2), NY)
             for a, total in ((0, hid), (1, gact)):
-                right = wt[a, lax.div(p, NY), pair].reshape(2 * KB, UN)
-                total[:size] += dot_nn(operand(a, p), right)
-
+                right = wt[a, pc, pl.ds(2 * py_, 2)].reshape(2 * KB, UN)
+                total[:size] += dot_nn(operand(a, pc, py_), right)
+
+    def hidden_ends(ks):
+        places = [rows(step(z, k, NZ)) for k in ks]
         for n, (k, at) in enumerate(zip(ks, places)):
             pz = step(z, k, NZ)
             h = hid[n * TZ : (n + 1) * TZ]
@@ -349,6 +362,7 @@
     turn(3)
     turn(5)
     w_hop1(4)
+    early = (0, 1, -1, 2, -2)
     land_all(zb[3])
     zb_step(4)
     cb_core(3)
@@ -356,14 +370,19 @@
     ya_hop2(4)
     ya_core(3)
     ya_core(-3)
+    land_blocks(early)
+    hidden_sums(early, (1, 2, 3))
     w_hop2(4)
     turn(4)
     w_far = push(ww.at[pl.ds(2 * (1 - c), 2), 0, :, :], wsib, sibling)
     ya_core(4)
-    hidden((0, 1, -1, 2, -2))
+    hidden_sums(early, (4,))
+    hidden_ends(early)
     land_all(zb[4])
     cb_core(4)
-    hidden((3, -3, 4))
+    land_blocks((3, -3, 4))
+    hidden_sums((3, -3, 4), (1, 2, 3, 4))
+    hidden_ends((3, -3, 4))
 
     def grad_parts(pc, a):
         left = pre_t if a == 0 else act_t
@@ -401,7 +420,7 @@
             push(part.at[prv, :, at, :], r2l.at[:, at, :], at_x(-1)),
         ]
 
-    def x_step3(q):
+    def x_sum(q):
         land_all(x2[q])
         at = piece(q)
         for a in range(2):
@@ -409,8 +428,13 @@
                 part[x, a, at, :].astype(F32)
                 + r2r[a, at, :].astype(F32)
                 + r2l[a, at, :].astype(F32)
-            )
-            red[a, at, :] = total.astype(BF)
+            ).astype(BF)
+            red[a, at, :] = total
+            v = total.astype(F32)
+            squares[...] += jnp.sum(v * v, axis=0, keepdims=True)
+
+    def x_spread(q):
+        at = piece(q)
         place = land.at[:, pl.ds(pl.multiple_of(z * UB + PIECES[q], 16), at.size), :]
         gz[q] = [
             push(red.at[:, at, cols(step(z, k, NZ))], place, at_z(k))
@@ -418,15 +442,9 @@
         ]
         gz_own[q] = move(red.at[:, at, cols(z)], place)
 
-    def squares(q, total):
-        gz_own[q].wait()
-        land_all(gz[q])
-        at = piece(q)
-        for a in range(2):
-            for n in range(NZ):
-                v = land[a, pl.ds(n * UB + at.start, at.size), :].astype(F32)
-                total = total + jnp.sum(v * v, axis=0, keepdims=True)
-        return total
+    def x_step3(q):
+        x_sum(q)
+        x_spread(q)
 
     pieces = (2, 1, 3, 0)
     size = NZ * XT
@@ -516,6 +534,7 @@
         else:
             ox[span(x * XT, XT), :] = total
 
+    squares[...] = jnp.zeros_like(squares)
     grad_parts(1 - xh, 0)
     for q in range(4):
         x_step1(q, 0)
@@ -531,11 +550,11 @@
     grad_parts(xh, 0)
     grad_parts(xh, 1)
     x_step2(0)
+    x_step2(1)
     y_step2(0)
-    x_step2(1)
+    x_step2(2)
     y_step1(3)
     y_step2(1)
-    x_step2(2)
     for q in (4, 5):
         x_step1(q, 0)
         x_step1(q, 1)
@@ -543,39 +562,27 @@
     y_step2(2)
     x_step3(1)
     y_step3(0)
+    z_step(0, 1)
     x_step2(3)
     y_step2(3)
     x_step3(2)
     y_step3(1)
-    z_step(0, 1)
     z_step(1, 1)
+    z_step(0, 2)
     x_step2(4)
     x_step2(5)
     y_step3(2)
-    z_step(0, 2)
+    z_step(2, 1)
     z_step(1, 2)
+    z_step(0, 3)
     x_step3(3)
-    total = squares(0, jnp.zeros((1, KB), F32))
-    total = squares(1, total)
+    z_step(2, 2)
     y_step3(3)
-    z_step(2, 1)
     z_step(3, 1)
-    z_step(0, 3)
-    z_step(1, 3)
-    x_step3(4)
-    x_step3(5)
-    total = squares(2, total)
-    z_step(2, 2)
-    z_step(3, 2)
-    z_step(0, 4)
-    z_step(1, 4)
-    total = squares(3, total)
-    z_step(2, 3)
-    z_step(3, 3)
-    total = squares(4, total)
-
-    total = squares(5, total)
-    value = jnp.sum(total, axis=1, keepdims=True)
+    x_sum(4)
+    x_sum(5)
+
+    value = jnp.sum(squares[...], axis=1, keepdims=True)
 
     def exchange(stage, me, targets, value):
         nb[stage, me] = jnp.broadcast_to(value, (8, 128))
@@ -589,25 +596,40 @@
         return total[:1, :1]
 
     norm = exchange(0, 2 * z + c, column, value)
+    z_step(1, 3)
+    z_step(2, 3)
+    x_spread(4)
+    x_spread(5)
+    z_step(3, 2)
+    z_step(0, 4)
+    z_step(1, 4)
+    z_step(2, 4)
+    value = collect(0, norm)
+    norm = exchange(1, 4 * x + y, plane, value)
+    z_step(3, 3)
     z_last(0)
     z_last(1)
-    z_step(2, 4)
+    z_last(2)
     z_step(3, 4)
-    value = collect(0, norm)
-    norm = exchange(1, 4 * x + y, plane, value)
-    down_out[...] = land[1]
-    z_last(2)
+    for q in gz:
+        gz_own[q].wait()
+        land_all(gz[q])
+    down_copy = move(land.at[1], down_out)
 
     @pl.loop(0, NZ)
     def _(t):
         at = span(t * UB, UB)
-        up_out[:, at] = land[0, at, :].T
-
+        up_t[:, at] = land[0, at, :].T
+
+    up_copy = move(up_t, up_out)
+    value = collect(1, norm)
+    sq_out[0, 0] = jnp.max(value)
+    scale_out[0, 0] = jnp.max(1.0 / jnp.sqrt(value / (2.0 * D * FF)))
     z_last(3)
     land_all(far_out)
     ig_out[...] = ox[...]
-    value = collect(1, norm)
-    sq_out[0, 0] = jnp.max(value)
+    down_copy.wait()
+    up_copy.wait()
 
     for copy in started:
         copy.wait_send()
@@ -616,16 +638,18 @@
 def on_device(inputs, cotangent, w_up, w_down):
     vmem = pl.BlockSpec(memory_space=pltpu.VMEM)
     hbm = pl.BlockSpec(memory_space=pl.ANY)
-    ig, up, down, total = pl.pallas_call(
+    smem = pl.BlockSpec(memory_space=pltpu.SMEM)
+    ig, up, down, total, scale = pl.pallas_call(
         kernel,
         out_shape=(
             jax.ShapeDtypeStruct((NX * XT, KB), BF),
             jax.ShapeDtypeStruct((KB, NZ * UB), BF),
             jax.ShapeDtypeStruct((NZ * UB, KB), BF),
             jax.ShapeDtypeStruct((1, 1), F32),
+            jax.ShapeDtypeStruct((1, 1), F32),
         ),
         in_specs=[hbm] * 4,
-        out_specs=(vmem, vmem, vmem, pl.BlockSpec(memory_space=pltpu.SMEM)),
+        out_specs=(vmem, hbm, hbm, smem, smem),
         scratch_shapes=[
             pltpu.VMEM((KB, NZ * UB), BF),
             pltpu.VMEM((2, NZ * UB, KB), BF),
@@ -656,6 +680,8 @@
             pltpu.VMEM((4, 4, XT, KB), BF),
             pltpu.VMEM((4, XT, KB), BF),
             pltpu.VMEM((NX * XT, KB), BF),
+            pltpu.VMEM((KB, NZ * UB), BF),
+            pltpu.VMEM((1, ROW), F32),
             pltpu.VMEM((2, 16, 8, 128), F32),
             pltpu.SemaphoreType.DMA((304,)),
             pltpu.SemaphoreType.DMA((304,)),
@@ -669,7 +695,7 @@
         ),
     )(inputs, cotangent, w_up, w_down)
     mean_square = total[0, 0] / jnp.float32(2.0 * D * FF)
-    scale = 1.0 / jnp.sqrt(mean_square)
+    scale = scale[0, 0]
     return ig, up.astype(F32) * scale, down.astype(F32) * scale, mean_square
 
 

time: 161 us -> 157 us (0.975)
  Pallas kernels: 155 us -> 149 us
    pallas_call x1, Pallas kernels: 155 us -> 149 us  [on_device(): pl.pallas_call(kernel, out_shape=(jax.ShapeDtypeStruct((NX * XT, KB), BF)...]
where the time goes in v4:
time: 157 us; the launch traced here: 156 us
  Pallas kernels  149 us (95%)
  other arithmetic  4.4 us (3%)
  between operations  2.41 us (2%)
    pallas_call x1, Pallas kernels, on_device(): pl.pallas_call(kernel, out_shape=(jax.ShapeDtypeStruct((NX * XT, KB), BF)...  149 us
    mul x2, other arithmetic, on_device(): return (ig, up.astype(F32) * scale, down.astype(F32) * scale, mean_square)  4.4 us

profile of v4, /device:TPU:1, one launch (start us, length us, event | category | flops | bytes accessed | tf_op | source)
XLA Modules:
  0.0 156.4 jit_solution(3261995104942145173)
XLA Ops:
  0.6 149.0 %shard_map.75 = (bf16[256,256]{1,0:T(8,128)(2,1)}, bf16[256,1024]{1,0:T(8,128)(2,1)}, bf16[1024,256]{1,0:T(8,128)(2,1)}, f32[1,1]{1,0:T(1,128)}, f32[1,1]{1,0:T(1,128)}) custom-call(bf16[256,256]{1,0:T(8,128)(2,1)} %x_in.1, bf16[256,256]{1,0:T(8,128)(2,1)} %dy_in.1, bf16[256,1024]{1,0:T(8,128)(2,1)} %wu_in.1, bf16[1024,256]{1,0:T(8,128)(2,1)} %wd_in.1), custom_call_target="tpu_custom_call" | custom-call | flops 11000000512 | bytes 8000000 | tf_op jit(solution)/shard_map/pallas_call | solution.py:642
  150.2 0.0 copy-start
  150.3 2.8 %convert_multiply_fusion.1 = f32[256,1024]{1,0:T(8,128)} fusion(bf16[256,1024]{1,0:T(8,128)(2,1)} %get-tuple-element.10, f32[]{:T(128)} %bitcast), kind=kLoop, calls=%fused_computation.1 | loop fusion | flops 524288 | bytes 1572868 | tf_op jit(solution)/shard_map/mul | solution.py:699
  153.0 0.0 copy-done
  153.0 0.0 copy-start.1
  153.0 1.6 %convert_multiply_fusion = f32[1024,256]{1,0:T(8,128)} fusion(bf16[1024,256]{1,0:T(8,128)(2,1)S(1)} %copy-done, f32[]{:T(128)} %bitcast), kind=kLoop, calls=%fused_computation | loop fusion | flops 524288 | bytes 1572868 | tf_op jit(solution)/shard_map/mul | solution.py:699
  154.7 0.0 copy-done.1
  154.7 0.7 copy.9
Async XLA Ops:
  150.2 2.8 %copy-start = (bf16[1024,256]{1,0:T(8,128)(2,1)S(1)}, bf16[1024,256]{1,0:T(8,128)(2,1)}, u32[]{:S(2)}) copy-start(bf16[1024,256]{1,0:T(8,128)(2,1)} %get-tuple-element.12) | copy-start | bytes 1572868
  153.0 1.6 %copy-start.1 = (bf16[256,256]{1,0:T(8,128)(2,1)S(1)}, bf16[256,256]{1,0:T(8,128)(2,1)}, u32[]{:S(2)}) copy-start(bf16[256,256]{1,0:T(8,128)(2,1)} %get-tuple-element.18) | copy-start | bytes 393220

commit v5 on v4

--- a/solution.py
+++ b/solution.py
@@ -48,7 +48,7 @@
 
 
 def kernel(
-    x_in, dy_in, wu_in, wd_in, ig_out, up_out, down_out, sq_out, scale_out,
+    x_in, dy_in, wu_in, wd_in, ig_out, up_out, down_out, sq_out,
     wu, ws, xy, ww, wt, wsib, hid, gact, act_t, pre, pre_t, pre_sib,
     part, r1r, r1l, r2r, r2l, red, land,
     py, y1r, y1l, y2r, y2l, ty, z_r, z_l, fz, ox, up_t, squares, nb,
@@ -263,7 +263,7 @@
             hid[:size] = jnp.zeros((size, UN), F32)
             gact[:size] = jnp.zeros((size, UN), F32)
 
-        @pl.loop(0, 2 * len(chunks))
+        @pl.loop(0, 2 * len(chunks), unroll=2)
         def _(p):
             pc = lax.rem(p, 2)
             py_ = lax.rem(late + chunks[0] + lax.div(p, 2), NY)
@@ -387,7 +387,7 @@
     def grad_parts(pc, a):
         left = pre_t if a == 0 else act_t
 
-        @pl.loop(0, NZ)
+        @pl.loop(0, NZ, unroll=4)
         def _(q):
             right = xy[
                 pc, lax.div(q, 2), :, span((2 * lax.rem(q, 2) + a) * KB, KB)
@@ -624,7 +624,6 @@
     up_copy = move(up_t, up_out)
     value = collect(1, norm)
     sq_out[0, 0] = jnp.max(value)
-    scale_out[0, 0] = jnp.max(1.0 / jnp.sqrt(value / (2.0 * D * FF)))
     z_last(3)
     land_all(far_out)
     ig_out[...] = ox[...]
@@ -639,17 +638,16 @@
     vmem = pl.BlockSpec(memory_space=pltpu.VMEM)
     hbm = pl.BlockSpec(memory_space=pl.ANY)
     smem = pl.BlockSpec(memory_space=pltpu.SMEM)
-    ig, up, down, total, scale = pl.pallas_call(
+    ig, up, down, total = pl.pallas_call(
         kernel,
         out_shape=(
             jax.ShapeDtypeStruct((NX * XT, KB), BF),
             jax.ShapeDtypeStruct((KB, NZ * UB), BF),
             jax.ShapeDtypeStruct((NZ * UB, KB), BF),
             jax.ShapeDtypeStruct((1, 1), F32),
-            jax.ShapeDtypeStruct((1, 1), F32),
         ),
         in_specs=[hbm] * 4,
-        out_specs=(vmem, hbm, hbm, smem, smem),
+        out_specs=(vmem, hbm, hbm, smem),
         scratch_shapes=[
             pltpu.VMEM((KB, NZ * UB), BF),
             pltpu.VMEM((2, NZ * UB, KB), BF),
@@ -695,7 +693,7 @@
         ),
     )(inputs, cotangent, w_up, w_down)
     mean_square = total[0, 0] / jnp.float32(2.0 * D * FF)
-    scale = scale[0, 0]
+    scale = 1.0 / jnp.sqrt(mean_square)
     return ig, up.astype(F32) * scale, down.astype(F32) * scale, mean_square
 
 

time: 157 us -> 155 us (0.987)
  Pallas kernels: 149 us -> 147 us
    pallas_call x1, Pallas kernels: 149 us -> 147 us  [on_device(): pl.pallas_call(kernel, out_shape=(jax.ShapeDtypeStruct((NX * XT, KB), BF)...]
where the time goes in v5:
time: 155 us; the launch traced here: 153 us
  Pallas kernels  147 us (95%)
  other arithmetic  3.23 us (2%)
  between operations  2.45 us (2%)
    pallas_call x1, Pallas kernels, on_device(): pl.pallas_call(kernel, out_shape=(jax.ShapeDtypeStruct((NX * XT, KB), BF)...  147 us
    mul x2, other arithmetic, on_device(): return (ig, up.astype(F32) * scale, down.astype(F32) * scale, mean_square)  3.23 us

profile of v5, /device:TPU:1, one launch (start us, length us, event | category | flops | bytes accessed | tf_op | source)
XLA Modules:
  0.0 152.9 jit_solution(13117228255281454252)
XLA Ops:
  0.6 146.5 %shard_map.75 = (bf16[256,256]{1,0:T(8,128)(2,1)}, bf16[256,1024]{1,0:T(8,128)(2,1)}, bf16[1024,256]{1,0:T(8,128)(2,1)}, f32[1,1]{1,0:T(1,128)}) custom-call(bf16[256,256]{1,0:T(8,128)(2,1)} %x_in.1, bf16[256,256]{1,0:T(8,128)(2,1)} %dy_in.1, bf16[256,1024]{1,0:T(8,128)(2,1)} %wu_in.1, bf16[1024,256]{1,0:T(8,128)(2,1)} %wd_in.1), custom_call_target="tpu_custom_call" | custom-call | flops 11000000512 | bytes 8000000 | tf_op jit(solution)/shard_map/pallas_call | solution.py:641
  147.8 0.0 copy-start
  147.8 2.2 %convert_multiply_fusion.1 = f32[256,1024]{1,0:T(8,128)} fusion(bf16[256,1024]{1,0:T(8,128)(2,1)} %get-tuple-element.9, f32[]{:T(128)S(6)} %sqrt.3), kind=kLoop, calls=%fused_computation.1 | loop fusion | flops 524288 | bytes 1572868 | tf_op jit(solution)/shard_map/mul | solution.py:697
  150.0 0.0 copy-done
  150.0 0.0 copy-start.1
  150.0 1.0 convert_multiply_fusion
  151.1 0.0 copy-done.1
  151.1 0.7 copy.9
Async XLA Ops:
  147.8 2.2 %copy-start = (bf16[1024,256]{1,0:T(8,128)(2,1)S(1)}, bf16[1024,256]{1,0:T(8,128)(2,1)}, u32[]{:S(2)}) copy-start(bf16[1024,256]{1,0:T(8,128)(2,1)} %get-tuple-element.11) | copy-start | bytes 1572868
  150.0 1.0 copy-start.1

commit v6 on v5

--- a/solution.py
+++ b/solution.py
@@ -228,7 +228,7 @@
         land_all(wx2[k])
         pz = step(z, -k, NZ)
 
-        @pl.loop(0, 2)
+        @pl.loop(0, 2, unroll=2)
         def _(pc):
             for a in range(2):
                 wt[a, pc, pz] = weight(a, pc, pz * KB).T
@@ -263,7 +263,7 @@
             hid[:size] = jnp.zeros((size, UN), F32)
             gact[:size] = jnp.zeros((size, UN), F32)
 
-        @pl.loop(0, 2 * len(chunks), unroll=2)
+        @pl.loop(0, 2 * len(chunks), unroll=2 * len(chunks))
         def _(p):
             pc = lax.rem(p, 2)
             py_ = lax.rem(late + chunks[0] + lax.div(p, 2), NY)

time: 155 us -> 153 us (0.987)
  Pallas kernels: 147 us -> 145 us
where the time goes in v6:
time: 153 us; the launch traced here: 152 us
  Pallas kernels  145 us (95%)
  other arithmetic  3.23 us (2%)
  between operations  2.45 us (2%)
    pallas_call x1, Pallas kernels, on_device(): pl.pallas_call(kernel, out_shape=(jax.ShapeDtypeStruct((NX * XT, KB), BF)...  145 us
    mul x2, other arithmetic, on_device(): return (ig, up.astype(F32) * scale, down.astype(F32) * scale, mean_square)  3.23 us

profile of v6, /device:TPU:1, one launch (start us, length us, event | category | flops | bytes accessed | tf_op | source)
XLA Modules:
  0.0 151.6 jit_solution(8076336338870386199)
XLA Ops:
  0.6 145.3 %shard_map.75 = (bf16[256,256]{1,0:T(8,128)(2,1)}, bf16[256,1024]{1,0:T(8,128)(2,1)}, bf16[1024,256]{1,0:T(8,128)(2,1)}, f32[1,1]{1,0:T(1,128)}) custom-call(bf16[256,256]{1,0:T(8,128)(2,1)} %x_in.1, bf16[256,256]{1,0:T(8,128)(2,1)} %dy_in.1, bf16[256,1024]{1,0:T(8,128)(2,1)} %wu_in.1, bf16[1024,256]{1,0:T(8,128)(2,1)} %wd_in.1), custom_call_target="tpu_custom_call" | custom-call | flops 11000000512 | bytes 8000000 | tf_op jit(solution)/shard_map/pallas_call | solution.py:641
  146.6 0.0 copy-start
  146.6 2.2 %convert_multiply_fusion.1 = f32[256,1024]{1,0:T(8,128)} fusion(bf16[256,1024]{1,0:T(8,128)(2,1)} %get-tuple-element.9, f32[]{:T(128)S(6)} %sqrt.3), kind=kLoop, calls=%fused_computation.1 | loop fusion | flops 524288 | bytes 1572868 | tf_op jit(solution)/shard_map/mul | solution.py:697
  148.8 0.0 copy-done
  148.8 0.0 copy-start.1
  148.8 1.0 convert_multiply_fusion
  149.8 0.0 copy-done.1
  149.8 0.7 copy.9
Async XLA Ops:
  146.6 2.2 %copy-start = (bf16[1024,256]{1,0:T(8,128)(2,1)S(1)}, bf16[1024,256]{1,0:T(8,128)(2,1)}, u32[]{:S(2)}) copy-start(bf16[1024,256]{1,0:T(8,128)(2,1)} %get-tuple-element.11) | copy-start | bytes 1572868
  148.8 1.0 copy-start.1
